TPU v7x, 128 devices: a whole 4x4x4 slice. The times are simulated.
128 devices in a mesh: seq: 32 (over x, y, core), head: 4 (over z).
Axes of the slice: x: 4, y: 4, z: 4, core: 2. Of those that a mesh axis runs over, the one named last changes fastest.
Arguments:
- tokens: bfloat16 [8192, 2048], P('seq'), may hold values from -6 to 6
- w_query: bfloat16 [2048, 2048], P(None, 'head'), may hold values from -0.125 to 0.125
- w_key: bfloat16 [2048, 2048], P(None, 'head'), may hold values from -0.125 to 0.125
- w_value: bfloat16 [2048, 2048], P(None, 'head'), may hold values from -0.125 to 0.125
- w_beta: bfloat16 [2048, 16], P(None, 'head'), may hold values from -0.125 to 0.125
- b_beta: float32 [16], P('head'), may hold values from -6 to 1
- d_out: bfloat16 [8192, 2048], P('seq', 'head'), may hold values from -6 to 6
Outputs:
- d_x: bfloat16 [8192, 2048], P('seq', 'head')
- grad_query: float32 [2048, 2048], P('seq', 'head')
- grad_key: float32 [2048, 2048], P('seq', 'head')
- grad_value: float32 [2048, 2048], P('seq', 'head')
- grad_wbeta: float32 [2048, 16], P('seq', 'head')
- grad_bbeta: float32 [16], P('head')
All inputs are finite; a program needn't handle non-finite values.
Results may differ from a plain program's by a relative error of at most 0.012.
Values may be sent and summed in bfloat16 or wider, within the bound.
No kernel may reach another device: no remote copies, remote signals or barrier semaphores. Data moves between devices by JAX's collectives and lax.ppermute only.
A program may use at most 128 MiB of HBM per device.

v0:
```python
import functools

import jax
import jax.numpy as jnp
from jax import lax
from jax.experimental import pallas as pl
from jax.experimental.pallas import tpu as pltpu
from jax.sharding import PartitionSpec as P

EPSILON = 1e-06
WIDTH = 128
ROWS = 256
PAIR = 2 * WIDTH
SIDE = 4
PACK = 3 * PAIR
FULL = PACK + WIDTH
VMEM = 24 * 2**20
BIG = 50 * 2**20
SLAB = 16
f32 = jnp.float32
bf16 = jnp.bfloat16
STATE = jnp.bfloat16
BASE = 8

NN = (((1,), (0,)), ((), ()))
NT = (((1,), (1,)), ((), ()))
TN = (((0,), (0,)), ((), ()))


def split(x):
    high = x.astype(bf16)
    return high, (x - high.astype(f32)).astype(bf16)


def one(a, b, dims):
    return lax.dot_general(a, b, dims, preferred_element_type=f32)


def dot(a, b, dims=NN):
    ah, al = a if isinstance(a, tuple) else split(a)
    bh, bl = b if isinstance(b, tuple) else split(b)
    total = one(ah, bh, dims)
    if bl is not None:
        total = total + one(ah, bl, dims)
    if al is not None:
        total = total + one(al, bh, dims)
    return total


def grid_iota(n):
    return (
        lax.broadcasted_iota(jnp.int32, (n, n), 0),
        lax.broadcasted_iota(jnp.int32, (n, n), 1),
    )


def inverses(lowers, row, col):
    n = lowers[0].shape[0]
    diff = row ^ col
    near = diff < BASE
    lane = lax.broadcasted_iota(jnp.int32, (BASE, n), 1) % BASE
    rank = lax.broadcasted_iota(jnp.int32, (BASE, n), 0)
    totals = []
    for lower in lowers:
        packed = jnp.where(near, lower, 0.0).reshape(n // BASE, BASE, n).sum(0)
        solved = jnp.where(lane == rank, 1.0, 0.0)
        for j in range(BASE - 1):
            factor = jnp.where(lane == j, packed, 0.0)
            if j:
                factor = pltpu.roll(factor, n - j, 1)
            step = 1
            while step < BASE:
                factor = factor + pltpu.roll(factor, step, 1)
                step *= 2
            solved = solved - factor * solved[j : j + 1, :]
        wide = jnp.broadcast_to(solved[None], (n // BASE, BASE, n)).reshape(n, n)
        totals.append(jnp.where(near, wide, 0.0))
    size = BASE
    while size < n // 2:
        mask = (diff >= size) & (diff < 2 * size)
        pieces = [split(t) for t in totals]
        inner = [dot(jnp.where(mask, w, 0.0), p) for w, p in zip(lowers, pieces)]
        totals = [t - dot(p, i) for t, p, i in zip(totals, pieces, inner)]
        size *= 2
    h = n // 2
    firsts = [split(t[:h, :h]) for t in totals]
    lasts = [split(t[h:, h:]) for t in totals]
    inner = [dot(w[h:, :h], p) for w, p in zip(lowers, firsts)]
    corners = [-dot(p, i) for p, i in zip(lasts, inner)]
    return [
        jnp.concatenate([t[:h], jnp.concatenate([c, t[h:, h:]], 1)], 0)
        for t, c in zip(totals, corners)
    ]


def merge_pair(first, second):
    d1, o1, a1 = first
    d2, o2, a2 = second
    s2 = split(d2)
    s1 = split(d1)
    return (
        d1 + d2 - dot(s1, s2),
        o1 + o2 - dot(o1, s2),
        a1 + a2 - dot(a2, s1, NT),
    )


def project(x, wq_ref, wk_ref, wv_ref, wb_ref):
    return [
        one(x, wq_ref[...], NN),
        one(x, wk_ref[...], NN),
        one(x, wv_ref[...], NN),
        one(x, wb_ref[...], NT),
    ]


def project_kernel(place_ref, x_ref, wq_ref, wk_ref, wv_ref, wb_ref, out_ref):
    parts = project(x_ref[...], wq_ref, wk_ref, wv_ref, wb_ref)
    for place, part in enumerate(parts):
        out_ref[:, place * PAIR : place * PAIR + part.shape[1]] = part


def local_kernel(core_ref, own_ref, x_ref, wq_ref, wk_ref, wv_ref, wb_ref, do_ref, sdo_ref, bb_ref,
                 saved_ref, solve_ref, gates_ref, maps_ref, send_ref):
    core = core_ref[0]
    row, col = grid_iota(ROWS)
    lane = lax.broadcasted_iota(jnp.int32, (ROWS, WIDTH), 1)
    own = [own_ref[:, i * PAIR : (i + 1) * PAIR] for i in range(3)]
    heads = wb_ref.shape[0]
    own.append(own_ref[:, 3 * PAIR : 3 * PAIR + heads])
    sib = project(x_ref[...], wq_ref, wk_ref, wv_ref, wb_ref)
    narrow = lax.broadcasted_iota(jnp.int32, (ROWS, heads), 1)
    cuts = (slice(0, WIDTH), slice(WIDTH, PAIR))
    cases = [(unit, head) for unit in range(2) for head in range(2)]
    every = range(4)
    parts = (own, sib)
    d_outs = [((do_ref, sdo_ref)[u][:, cuts[h]], None) for u, h in cases]
    vs = [parts[u][2][:, cuts[h]] for u, h in cases]
    qns, kns, betas = [], [], []
    for unit, head in cases:
        q, k = (parts[unit][i][:, cuts[head]] for i in (0, 1))
        rq = lax.rsqrt(jnp.sum(q * q, 1, keepdims=True) + EPSILON)
        rk = lax.rsqrt(jnp.sum(k * k, 1, keepdims=True) + EPSILON)
        z = parts[unit][3]
        logit = jnp.sum(jnp.where(narrow == 2 * core + head, z, 0.0), 1, keepdims=True)
        beta = 2.0 * jax.nn.sigmoid(logit + bb_ref[2 * core + head])
        case = unit * 2 + head
        gates_ref[case] = jnp.where(lane == 0, beta, jnp.where(lane == 1, rq, rk))
        qns.append(q * rq)
        kns.append(k * rk)
        betas.append(beta)
    for i in every:
        saved_ref[i, 0] = qns[i]
        saved_ref[i, 1] = kns[i]
    ks = [split(kn) for kn in kns]
    grams = [jnp.where(row > col, dot(k, k, NT), 0.0) for k in ks]
    scores = [split(jnp.where(row >= col, dot(q, k, NT), 0.0)) for q, k in zip(qns, ks)]
    solves = inverses([beta * gram for beta, gram in zip(betas, grams)], row, col)
    solves = [split(x) for x in solves]
    wus = [
        split(dot(solves[i], jnp.concatenate([betas[i] * kns[i], betas[i] * vs[i]], 1)))
        for i in every
    ]
    pairs = [dot(wus[i], ks[i], TN) for i in every]
    reads = [
        qns[i] - dot(scores[i], (wus[i][0][:, :WIDTH], wus[i][1][:, :WIDTH])) for i in every
    ]
    adjoints = [dot(d_outs[i], reads[i], TN) for i in every]
    for i in every:
        maps_ref[i, 0] = pairs[i][:WIDTH]
        maps_ref[i, 1] = pairs[i][WIDTH:]
        maps_ref[i, 2] = adjoints[i]
        saved_ref[i, 2] = vs[i]
        for half in range(2):
            solve_ref[i, half] = solves[i][half]
            solve_ref[i, 2 + half] = wus[i][half]
    early = core == 0
    for head in range(2):
        mine = (pairs[head][:WIDTH], pairs[head][WIDTH:], adjoints[head])
        theirs = (pairs[2 + head][:WIDTH], pairs[2 + head][WIDTH:], adjoints[2 + head])
        first = [jnp.where(early, a, b) for a, b in zip(mine, theirs)]
        second = [jnp.where(early, b, a) for a, b in zip(mine, theirs)]
        step, offset, adjoint = merge_pair(first, second)
        send_ref[head, 0] = step.astype(STATE)
        send_ref[head, 1] = offset.astype(STATE)
        send_ref[head, 2] = adjoint.astype(STATE)


def by_core(kernel, name, core, args, halves, shapes, flops, nbytes, vmem):
    def whole(shape):
        return pl.BlockSpec(shape, lambda i, c: (0,) * len(shape))

    specs = [
        pl.BlockSpec((a.shape[0], PAIR), lambda i, c: (0, c[0]))
        if n in halves
        else (whole(a.shape) if a.ndim > 1 else pl.BlockSpec(memory_space=pltpu.SMEM))
        for n, a in enumerate(args)
    ]
    return pl.pallas_call(
        kernel,
        grid_spec=pltpu.PrefetchScalarGridSpec(
            num_scalar_prefetch=1,
            grid=(1,),
            in_specs=specs,
            out_specs=[whole(s.shape) for s in shapes],
        ),
        out_shape=shapes,
        compiler_params=pltpu.CompilerParams(vmem_limit_bytes=vmem),
        cost_estimate=pl.CostEstimate(flops=flops, bytes_accessed=nbytes, transcendentals=0),
        name=name,
    )(core, *args)


def extra_kernel(core_ref, saved_ref, solve_ref, do_ref, sdo_ref, out_ref):
    row, col = grid_iota(ROWS)
    every = range(4)
    d_outs = [((do_ref, sdo_ref)[i // 2][:, (i % 2) * WIDTH : (i % 2 + 1) * WIDTH], None) for i in every]
    kns = [saved_ref[i, 1] for i in every]
    ks = [split(kn) for kn in kns]
    grams = [jnp.where(row > col, dot(k, k, NT), 0.0) for k in ks]
    scores = [jnp.where(row >= col, dot(saved_ref[i, 0], ks[i], NT), 0.0) for i in every]
    gwus = [dot(grams[i], (solve_ref[i, 2], solve_ref[i, 3])) for i in every]
    pulled = [dot(scores[i], d_outs[i], TN) for i in every]
    backs = [
        dot((solve_ref[i, 0], solve_ref[i, 1]), jnp.concatenate([kns[i], pulled[i]], 1), TN)
        for i in every
    ]
    for i in every:
        out_ref[i, 0] = kns[i] - gwus[i][:, :WIDTH]
        out_ref[i, 1] = saved_ref[i, 2] - gwus[i][:, WIDTH:]
        out_ref[i, 2] = backs[i][:, :WIDTH]
        out_ref[i, 3] = backs[i][:, WIDTH:]


def flip_kernel(own_ref, sib_ref, after_ref, out_ref):
    step = pl.program_id(0)
    rows = out_ref.shape[3]
    for source, cut in ((own_ref, slice(0, ROWS)), (sib_ref, slice(ROWS, 2 * ROWS))):
        turned = source[...].T
        for j in range(SIDE):
            base = 2 * j * rows
            out_ref[0, j, step, :, cut] = turned[base : base + rows]
            out_ref[1, step, j, :, cut] = turned[base + rows : base + 2 * rows]


def compose_kernel(place_ref, own_ref, one_ref, two_ref, three_ref, after_ref, extra_ref, span_ref, *refs):
    sends, maps_ref = refs[:-1], refs[-1]
    y, x = place_ref[1], place_ref[2]
    for k, ref in enumerate((own_ref, one_ref, two_ref, three_ref)):
        maps_ref[lax.rem(y - k + SIDE, SIDE)] = ref[...]
    last = y == SIDE - 1
    for head in range(2):
        a, b, c, d = ([maps_ref[j, head, i].astype(f32) for i in range(3)] for j in range(SIDE))
        low = merge_pair(a, b)
        high = merge_pair(c, d)
        extra = merge_pair(
            [jnp.where(last, p, q) for p, q in zip(low, b)],
            [jnp.where(last, p, q) for p, q in zip(c, high)],
        )
        step, offset, adjoint = merge_pair(low, high)
        for i in (0, 1):
            before = jnp.where(y == 1, a[i], jnp.where(y == 2, low[i], extra[i]))
            span_ref[head, i] = jnp.where(y == 0, 0.0, before)
        for i, place in ((0, 2), (2, 3)):
            behind = jnp.where(y == 2, d[i], jnp.where(y == 1, high[i], extra[i]))
            span_ref[head, place] = jnp.where(last, 0.0, behind)
        for k, out in enumerate(sends, 1):
            out[head, 0] = step.astype(STATE)
            out[head, 1] = jnp.where(x + k < SIDE, offset, adjoint).astype(STATE)


def back_kernel(place_ref, saved_ref, extra_ref, gates_ref, maps_ref, do_ref, sdo_ref, span_ref, one_ref,
                two_ref, three_ref, grads_ref, sums_ref):
    core, x = place_ref[0], place_ref[2]
    rows_of = {1: one_ref, 2: two_ref, 3: three_ref}
    early = core == 0
    row, col = grid_iota(ROWS)
    lane = lax.broadcasted_iota(jnp.int32, (ROWS, WIDTH), 1)
    rank = lax.broadcasted_iota(jnp.int32, (SLAB, WIDTH), 0)
    shares = [jnp.zeros((ROWS, WIDTH), f32) for _ in range(2)]
    sums = jnp.zeros((SLAB, WIDTH), f32)
    for head in range(2):
        start = jnp.zeros((WIDTH, WIDTH), f32)
        later = jnp.zeros((WIDTH, WIDTH), f32)
        for k in (3, 2, 1):
            moved = start + rows_of[k][head, 1].astype(f32)
            if k < 3:
                moved = moved - dot(start, (rows_of[k][head, 0], None))
            start = jnp.where(x >= k, moved, start)
        for k in (1, 2, 3):
            moved = later + rows_of[k][head, 1].astype(f32)
            if k > 1:
                moved = moved - dot(later, (rows_of[k][head, 0], None), NT)
            later = jnp.where(x < k, moved, later)
        start = start + span_ref[head, 1] - dot(start, span_ref[head, 0])
        later = later + span_ref[head, 3] - dot(later, span_ref[head, 2], NT)
        mine = [maps_ref[head, i] for i in range(3)]
        theirs = [maps_ref[2 + head, i] for i in range(3)]
        d1, o1 = (jnp.where(early, mine[i], theirs[i]) for i in (0, 1))
        d2, a2 = (jnp.where(early, theirs[i], mine[i]) for i in (0, 2))
        middle = start + o1 - dot(start, d1)
        inner = later + a2 - dot(later, d2, NT)
        states = (jnp.where(early, start, middle), jnp.where(early, middle, start))
        duals = (jnp.where(early, inner, later), jnp.where(early, later, inner))
        for unit in range(2):
            case = 2 * unit + head
            d_out = (do_ref, sdo_ref)[unit][:, head * WIDTH : (head + 1) * WIDTH]
            qn, kn = saved_ref[case, 0], saved_ref[case, 1]
            gates = gates_ref[case]
            beta, rq, rk = gates[:, 0:1], gates[:, 1:2], gates[:, 2:3]
            state, dual = split(states[unit]), split(duals[unit])
            error = extra_ref[case, 1] - dot(extra_ref[case, 0], state, NT)
            y = extra_ref[case, 3] + dot(extra_ref[case, 2], dual, NT)
            update = split(beta * error)
            dv = beta * y
            dvb = dv.astype(bf16)
            ks, qs = split(kn), split(qn)
            pulls = jnp.concatenate([d_out, dvb], 0)
            products = dot((pulls, None), update, NT)
            dm = jnp.where(row >= col, products[:ROWS], 0.0).astype(bf16)
            dn = jnp.where(row > col, products[ROWS:], 0.0).astype(bf16)
            lefts = dot((jnp.concatenate([dm, dn], 0), None), ks)
            rights = dot((pulls, None), state)
            both = tuple(jnp.concatenate([a, b], 0) for a, b in zip(qs, ks))
            dqn = rights[:ROWS] + lefts[:ROWS]
            dkn = (
                dot((jnp.concatenate([dm, -dn], 0), None), both, TN)
                + dot((update[0], None), dual)
                - lefts[ROWS:]
                - rights[ROWS:]
            )
            dq = rq * (dqn - qn * jnp.sum(qn * dqn, 1, keepdims=True))
            dk = rk * (dkn - kn * jnp.sum(kn * dkn, 1, keepdims=True))
            dz = jnp.sum(y * error, 1, keepdims=True) * beta * (1.0 - 0.5 * beta)
            for place, grad in enumerate((dq, dk, dv)):
                base = place * PAIR + head * WIDTH
                grads_ref[unit, :, base : base + WIDTH] = grad.astype(bf16)
            shares[unit] = shares[unit] + jnp.where(lane == 2 * core + head, dz, 0.0)
            sums = sums + jnp.where(rank == 4 + 2 * core + head, jnp.sum(dz, 0, keepdims=True), 0.0)
    for unit in range(2):
        grads_ref[unit, :, PACK:] = shares[unit].astype(bf16)
    sums_ref[...] = sums


def weights_kernel(away, place_ref, flipped_ref, grads_ref, sums_ref, *outs):
    rows = flipped_ref.shape[3]
    span = SIDE * rows
    grads = grads_ref[:, :, :PACK].reshape(2 * ROWS, PACK)
    shares = grads_ref[:, :, PACK:].reshape(2 * ROWS, WIDTH).T[:SLAB]
    lefts = [
        flipped_ref[0, lax.rem(place_ref[4 + away] + k, SIDE)].reshape(span, 2 * ROWS)
        for k in range(SIDE)
    ]
    lefts = jnp.concatenate(lefts, 0)
    total = one(lefts, grads, NN).astype(bf16)
    high, low = split(one(shares, lefts, NT) + sums_ref[:, 0:1])
    for k in range(SIDE):
        cut = slice(k * span, (k + 1) * span)
        outs[k][:span] = total[cut]
        outs[k][span:, :span] = high[:, cut]
        outs[k][span:, span : 2 * span] = low[:, cut]
        outs[k][span:, 2 * span :] = jnp.zeros((SLAB, PACK - 2 * span), bf16)
    if away:
        outs[SIDE][...] = grads_ref[1]


def weights_pass(name, away, place, flipped, grads, sums):
    rows = flipped.shape[3]
    shapes = [jax.ShapeDtypeStruct((SIDE * rows + SLAB, PACK), bf16)] * SIDE
    if away:
        shapes.append(jax.ShapeDtypeStruct(grads.shape[1:], bf16))

    def whole(shape):
        return pl.BlockSpec(shape, lambda k, p: (0,) * len(shape))

    return pl.pallas_call(
        functools.partial(weights_kernel, away),
        grid_spec=pltpu.PrefetchScalarGridSpec(
            num_scalar_prefetch=1,
            grid=(1,),
            in_specs=[
                pl.BlockSpec(
                    (1,) + flipped.shape[1:],
                    lambda k, p: (1 - p[0] if away else p[0], 0, 0, 0, 0),
                ),
                whole(grads.shape),
                whole(sums.shape),
            ],
            out_specs=[whole(s.shape) for s in shapes],
        ),
        out_shape=shapes,
        compiler_params=pltpu.CompilerParams(vmem_limit_bytes=VMEM),
        cost_estimate=pl.CostEstimate(flops=10**9, bytes_accessed=4 * 10**6, transcendentals=0),
        name=name,
    )(place, flipped, grads, sums)


def fair_sum(terms):
    return (terms[0] + terms[3]) + (terms[1] + terms[2])


def middle_kernel(place_ref, *refs):
    inputs, outs = refs[: 2 * SIDE], refs[2 * SIDE + 1 :]
    base = place_ref[5]
    rows = outs[0].shape[1] - SLAB
    span = SIDE * rows
    for pair in range(2):
        group = inputs[pair * SIDE : (pair + 1) * SIDE]
        slab = fair_sum(
            [ref[span:, :span].astype(f32) + ref[span:, span : 2 * span].astype(f32) for ref in group]
        )
        for k in range(SIDE):
            slot = lax.rem(base + k, SIDE)
            place = pl.ds(pl.multiple_of(slot * rows, rows), rows)
            total = group[0][place, :].astype(f32)
            for ref in group[1:]:
                total = total + ref[place, :].astype(f32)
            kind = outs[k].dtype
            outs[k][pair, :rows] = total.astype(kind)
            turned = pltpu.roll(slab, lax.rem(span - slot * rows, span), 1)[:, :WIDTH]
            high = turned.astype(bf16).astype(f32)
            outs[k][pair, rows:, :WIDTH] = high.astype(kind)
            outs[k][pair, rows:, WIDTH : 2 * WIDTH] = (turned - high).astype(bf16).astype(kind)
            outs[k][pair, rows:, 2 * WIDTH :] = jnp.zeros((SLAB, PACK - 2 * WIDTH), kind)


def total_kernel(core_ref, own_ref, one_ref, two_ref, three_ref, *outs):
    early = core_ref[0] == 0
    rows = own_ref.shape[1] - SLAB
    sums = []
    tails = []
    refs = (own_ref, one_ref, two_ref, three_ref)
    for pair in range(2):
        total = own_ref[pair, :rows]
        for ref in refs[1:]:
            total = total + ref[pair, :rows].astype(f32)
        sums.append(total)
        slabs = [ref[pair, rows:, : 2 * WIDTH].astype(f32) for ref in refs]
        tails.append(fair_sum([t[:, :WIDTH] + t[:, WIDTH:] for t in slabs]))
    outs[3][...] = tails[0] + tails[1]
    low = jnp.where(early, sums[0], sums[1])
    high = jnp.where(early, sums[1], sums[0])
    for place, out in enumerate(outs[:3]):
        cut = slice(place * PAIR, (place + 1) * PAIR)
        out[:, :PAIR] = low[:, cut]
        out[:, PAIR:] = high[:, cut]


def call(name, kernel, scalars, args, shapes, scratch=(), idle=(), flops=0, nbytes=0):
    def whole(shape):
        return pl.BlockSpec(shape, lambda i, p: (0,) * len(shape))

    return pl.pallas_call(
        kernel,
        grid_spec=pltpu.PrefetchScalarGridSpec(
            num_scalar_prefetch=1,
            grid=(1,),
            in_specs=[whole(a.shape) for a in args]
            + [pl.BlockSpec(memory_space=pl.ANY)] * len(idle),
            out_specs=[whole(s.shape) for s in shapes],
            scratch_shapes=list(scratch),
        ),
        out_shape=shapes,
        compiler_params=pltpu.CompilerParams(vmem_limit_bytes=VMEM),
        cost_estimate=pl.CostEstimate(flops=flops, bytes_accessed=nbytes, transcendentals=0),
        name=name,
    )(scalars, *args, *idle)


def input_kernel(place_ref, mine_ref, other_ref, wq_ref, wk_ref, wv_ref, wb_ref, after_ref, *outs):
    core, step = place_ref[0], pl.program_id(0)
    near = pl.ds(pl.multiple_of(core * PAIR, PAIR), PAIR)
    far = pl.ds(pl.multiple_of((1 - core) * PAIR, PAIR), PAIR)
    shares = (mine_ref[0, :, PACK:] + other_ref[:, PACK:])[:, : wb_ref.shape[0]]
    total = one(shares, wb_ref[...], NN)
    for place, w_ref in enumerate((wq_ref, wk_ref, wv_ref)):
        cut = slice(place * PAIR, (place + 1) * PAIR)
        total = total + one(mine_ref[0, :, cut], w_ref[:, near], NT)
        total = total + one(other_ref[:, cut], w_ref[:, far], NT)
    total = total.astype(bf16)
    for k, out in enumerate(outs):

        @pl.when(step == k)
        def _():
            out[...] = total


def per_device(tokens, w_query, w_key, w_value, w_beta, b_beta, d_out):
    depth = tokens.shape[1]
    index = lax.axis_index("seq")
    group = lax.axis_index("head")
    core = index % 2
    chip = index // 2
    y, x = chip % SIDE, chip // SIDE
    first, second = jnp.where(core == 0, y, x), jnp.where(core == 0, x, y)
    place = jnp.stack([core, y, x, group, first, second])
    seq = lax.axis_size("seq")
    ring = lax.axis_size("head")
    sibling = [(i, i ^ 1) for i in range(seq)]

    def swap(x):
        return lax.ppermute(x, "seq", sibling)

    other_tokens = swap(tokens)
    do_other = swap(d_out)
    wb = w_beta.T

    (projected,) = by_core(
        project_kernel,
        "project",
        place,
        [tokens, w_query, w_key, w_value, wb],
        (1, 2, 3),
        [jax.ShapeDtypeStruct((ROWS, PACK + WIDTH), f32)],
        10**9,
        5 * 10**6,
        BIG,
    )
    saved, solved, gates, own_maps, send = by_core(
        local_kernel,
        "local",
        place,
        [projected, other_tokens, w_query, w_key, w_value, wb, d_out, do_other, b_beta],
        (2, 3, 4, 6, 7),
        [
            jax.ShapeDtypeStruct((4, 3, ROWS, WIDTH), f32),
            jax.ShapeDtypeStruct((4, 4, ROWS, ROWS), bf16),
            jax.ShapeDtypeStruct((4, ROWS, WIDTH), f32),
            jax.ShapeDtypeStruct((4, 3, WIDTH, WIDTH), f32),
            jax.ShapeDtypeStruct((2, 3, WIDTH, WIDTH), STATE),
        ],
        10**10,
        10**7,
        BIG,
    )
    (extra,) = by_core(
        extra_kernel,
        "extra",
        place,
        [saved, solved, d_out, do_other],
        (2, 3),
        [jax.ShapeDtypeStruct((4, 4, ROWS, WIDTH), f32)],
        10**10,
        5 * 10**6,
        VMEM,
    )
    idle = pl.BlockSpec(memory_space=pl.ANY)

    def along(k, axis):
        route = []
        for i in range(seq):
            x, y, c = i // (2 * SIDE), i // 2 % SIDE, i % 2
            if axis(c):
                x = (x + k) % SIDE
            else:
                y = (y + k) % SIDE
            route.append((i, (x * SIDE + y) * 2 + c))
        return route

    def shift(block, k, axis):
        return lax.ppermute(block, "seq", along(k, axis))

    rows = depth // seq
    block = depth // SIDE
    layout = (2, SIDE, SIDE, rows, 2 * ROWS)
    flipped = pl.pallas_call(
        flip_kernel,
        grid=(SIDE,),
        in_specs=[pl.BlockSpec((ROWS, block), lambda i: (0, i))] * 2 + [idle],
        out_specs=pl.BlockSpec(layout, lambda i: (0,) * 5),
        out_shape=jax.ShapeDtypeStruct(layout, bf16),
        compiler_params=pltpu.CompilerParams(vmem_limit_bytes=VMEM),
        cost_estimate=pl.CostEstimate(flops=0, bytes_accessed=8 * 10**6, transcendentals=0),
        name="flip",
    )(tokens, other_tokens, send)

    far = {k: shift(send, k, lambda c: False) for k in (1, 3, 2)}
    part = (2, 2, WIDTH, WIDTH)
    span, *sends = call(
        "compose",
        compose_kernel,
        place,
        [send, far[1], far[2], far[3]],
        [jax.ShapeDtypeStruct((2, 4, WIDTH, WIDTH), f32)]
        + [jax.ShapeDtypeStruct(part, STATE)] * (SIDE - 1),
        scratch=[pltpu.VMEM((SIDE, 2, 3, WIDTH, WIDTH), STATE)],
        idle=[flipped, extra],
        flops=10**9,
    )
    far = {k: shift(sends[k - 1], k, lambda c: True) for k in (1, 3, 2)}

    grads, sums = by_core(
        back_kernel,
        "back",
        place,
        [saved, extra, gates, own_maps, d_out, do_other, span, far[1], far[2], far[3]],
        (4, 5),
        [
            jax.ShapeDtypeStruct((2, ROWS, FULL), bf16),
            jax.ShapeDtypeStruct((SLAB, WIDTH), f32),
        ],
        4 * 10**9,
        8 * 10**6,
        VMEM,
    )

    def across(k):
        return [(i, j ^ 1) for i, j in along(k, lambda c: c == 0)]

    *give, relay = weights_pass("give", 1, place, flipped, grads, sums)
    given = [lax.ppermute(give[k], "seq", across(k)) for k in (0, 1, 3, 2)]
    other_grads = swap(relay)
    keep = weights_pass("keep", 0, place, flipped, grads, sums)
    kept = [keep[0]] + [shift(keep[k], k, lambda c: c == 1) for k in (1, 3, 2)]

    width = depth // ring

    def full(shape):
        return pl.BlockSpec(shape, lambda i, p: (0,) * len(shape))

    def rows_at(columns):
        return pl.BlockSpec((width, columns), lambda i, p: (lax.rem(i + p[3], ring), 0))

    shifted = pl.pallas_call(
        input_kernel,
        grid_spec=pltpu.PrefetchScalarGridSpec(
            num_scalar_prefetch=1,
            grid=(ring,),
            in_specs=[full((1, ROWS, FULL)), full((ROWS, FULL))]
            + [rows_at(w_query.shape[1])] * 3
            + [
                pl.BlockSpec((wb.shape[0], width), lambda i, p: (0, lax.rem(i + p[3], ring))),
                idle,
            ],
            out_specs=[full((ROWS, width))] * ring,
        ),
        out_shape=[jax.ShapeDtypeStruct((ROWS, width), bf16)] * ring,
        compiler_params=pltpu.CompilerParams(vmem_limit_bytes=VMEM),
        cost_estimate=pl.CostEstimate(
            flops=4 * 10**10, bytes_accessed=8 * 10**6, transcendentals=0
        ),
        name="inputs",
    )(place, grads, other_grads, w_query, w_key, w_value, wb, keep[1])

    arrived = [
        lax.ppermute(shifted[k], "head", [(i, (i + k) % ring) for i in range(ring)])
        for k in range(1, ring)
    ]
    d_x = shifted[0].astype(f32)
    for piece in arrived:
        d_x = d_x + piece.astype(f32)
    d_x = d_x.astype(bf16)

    message = (2, rows + SLAB, PACK)
    passed = call(
        "middle",
        middle_kernel,
        place,
        [*kept, *given],
        [jax.ShapeDtypeStruct(message, f32)]
        + [jax.ShapeDtypeStruct(message, bf16)] * (SIDE - 1),
        idle=[shifted[0]],
    )
    final = [shift(passed[k], k, lambda c: c == 0) for k in (1, 3, 2)]
    grad_query, grad_key, grad_value, tail = call(
        "total",
        total_kernel,
        place,
        [passed[0], *final],
        [jax.ShapeDtypeStruct((rows, 2 * PAIR), f32)] * 3
        + [jax.ShapeDtypeStruct((SLAB, WIDTH), f32)],
    )
    heads = w_beta.shape[1]
    grad_bbeta = jnp.where(core == 0, tail, swap(tail))[4 : 4 + heads, 0]
    return (d_x, grad_query, grad_key, grad_value, tail[:heads, :rows].T, grad_bbeta)


def solution(mesh):
    columns = P(None, "head")
    both = P("seq", "head")
    return jax.shard_map(
        per_device,
        mesh=mesh,
        in_specs=(P("seq", None), columns, columns, columns, columns, P("head"), both),
        out_specs=(both, both, both, both, both, P("head")),
        check_vma=False,
    )
```

profile of v0, /device:TPU:0, one launch (start us, length us, event | category | flops | bytes accessed | tf_op | source)
XLA Modules:
  0.0 101.0 jit_solution(2583571048645986093)
XLA Ops:
  0.7 0.5 collective-permute-start.1
  1.3 1.2 %copy-done = bf16[256,2048]{1,0:T(8,128)(2,1)S(1)} copy-done((bf16[256,2048]{1,0:T(8,128)(2,1)S(1)}, bf16[256,2048]{1,0:T(8,128)(2,1)}, u32[]{:S(2)}) %copy-start) | copy-done | bytes 1048600
  2.5 1.6 %copy-done.2 = bf16[2048,512]{1,0:T(8,128)(2,1)S(1)} copy-done((bf16[2048,512]{1,0:T(8,128)(2,1)S(1)}, bf16[2048,512]{1,0:T(8,128)(2,1)}, u32[]{:S(2)}) %copy-start.2) | copy-done | bytes 2097176
  4.1 0.7 copy-done.6
  4.8 3.4 %project.1.own_ref = f32[256,896]{1,0:T(8,128)S(1)} custom-call(s32[6]{0:T(128)S(1)} %stack.27.place_ref.core_ref, bf16[256,2048]{1,0:T(8,128)(2,1)S(1)} %copy-done, bf16[2048,512]{1,0:T(8,128)(2,1)S(1)} %copy-done.2, bf16[2048,512]{1,0:T(8,128)(2,1)} %wk_ref.5, bf16[2048,512]{1,0:T(8,128)(2,1)} %wv_ref.5, bf16[4,2048]{1,0:T(4,128)(2,1)S(1)} %bitcast.9), custom_call_target="tpu_custom_call" | custom-call | flops 1000000000 | bytes 5000000 | tf_op jit(solution)/shard_map/project/pallas_call | solution.py:199
  8.3 10.2 %local.1 = (f32[4,3,256,128]{3,2,1,0:T(8,128)}, bf16[4,4,256,256]{3,2,1,0:T(8,128)(2,1)}, f32[4,256,128]{2,1,0:T(8,128)S(1)}, f32[4,3,128,128]{3,2,1,0:T(8,128)S(1)}, bf16[2,3,128,128]{3,2,1,0:T(8,128)(2,1)S(1)}) custom-call(s32[6]{0:T(128)S(1)} %stack.27.place_ref.core_ref, f32[256,896]{1,0:T(8,128)S(1)} %project.1.own_ref, ...), custom_call_target="tpu_custom_call" | custom-call | flops 10000000000 | bytes 10000000 | tf_op jit(solution)/shard_map/local/pallas_call | solution.py:199
  18.5 3.1 %collective-permute-start.4 = (bf16[2,3,128,128]{3,2,1,0:T(8,128)(2,1)S(1)}, bf16[2,3,128,128]{3,2,1,0:T(8,128)(2,1)S(1)}, u32[]{:S(2)}, u32[]{:S(2)}) collective-permute-start(bf16[2,3,128,128]{3,2,1,0:T(8,128)(2,1)S(1)} %get-tuple-element.42.after_ref.own_ref), channel_id=1, source_target_pairs={{0,24},{4,28},{8,0},{12,4},{16,8},{20,12},{24,16},{28,20},{32,56},... | collective-permute-start | bytes 589832 | tf_op jit(solution)/shard_map/ppermute | solution.py:561
  21.6 0.6 collective-permute-start.3
  22.2 1.0 collective-permute-start.2
  23.2 1.4 %copy-done.10 = f32[4,3,256,128]{3,2,1,0:T(8,128)S(1)} copy-done((f32[4,3,256,128]{3,2,1,0:T(8,128)S(1)}, f32[4,3,256,128]{3,2,1,0:T(8,128)}, u32[]{:S(2)}) %copy-start.10) | copy-done | bytes 1572888
  24.6 1.6 %copy-done.11 = bf16[4,4,256,256]{3,2,1,0:T(8,128)(2,1)S(1)} copy-done((bf16[4,4,256,256]{3,2,1,0:T(8,128)(2,1)S(1)}, bf16[4,4,256,256]{3,2,1,0:T(8,128)(2,1)}, u32[]{:S(2)}) %copy-start.11) | copy-done | bytes 2097176
  26.2 2.7 %extra.1.extra_ref = f32[4,4,256,128]{3,2,1,0:T(8,128)S(1)} custom-call(s32[6]{0:T(128)S(1)} %stack.27.place_ref.core_ref, f32[4,3,256,128]{3,2,1,0:T(8,128)S(1)} %copy-done.10, bf16[4,4,256,256]{3,2,1,0:T(8,128)(2,1)S(1)} %copy-done.11, bf16[256,512]{1,0:T(8,128)(2,1)S(1)} %copy-done.8, bf16[256,512]{1,0:T(8,128)(2,1)S(1)} %collective-permute-done.1.sdo_ref), custom_call_target="tpu_custom_call" | custom-call | flops 10000000000 | bytes 5000000 | tf_op jit(solution)/shard_map/extra/pallas_call | solution.py:199
  28.9 1.0 flip.1.after_ref.flipped_ref
  29.9 0.4 collective-permute-done.4.three_ref
  30.2 0.7 collective-permute-done.3.two_ref
  30.9 3.0 %collective-permute-done.2.one_ref = bf16[2,3,128,128]{3,2,1,0:T(8,128)(2,1)S(1)} collective-permute-done((bf16[2,3,128,128]{3,2,1,0:T(8,128)(2,1)S(1)}, bf16[2,3,128,128]{3,2,1,0:T(8,128)(2,1)S(1)}, u32[]{:S(2)}, u32[]{:S(2)}) %collective-permute-start.2) | collective-permute-done | bytes 196640 | tf_op jit(solution)/shard_map/ppermute | solution.py:561
  33.9 1.9 %compose.1 = (f32[2,4,128,128]{3,2,1,0:T(8,128)S(1)}, bf16[2,2,128,128]{3,2,1,0:T(8,128)(2,1)S(1)}, bf16[2,2,128,128]{3,2,1,0:T(8,128)(2,1)S(1)}, bf16[2,2,128,128]{3,2,1,0:T(8,128)(2,1)S(1)}) custom-call(s32[6]{0:T(128)S(1)} %stack.27.place_ref.core_ref, bf16[2,3,128,128]{3,2,1,0:T(8,128)(2,1)S(1)} %get-tuple-element.42.after_ref.own_ref, ...), custom_call_target="tpu_custom_call" | custom-call | flops 1000000000 | tf_op jit(solution)/shard_map/compose/pallas_call | solution.py:453
  35.8 1.6 %collective-permute-start.5 = (bf16[2,2,128,128]{3,2,1,0:T(8,128)(2,1)S(1)}, bf16[2,2,128,128]{3,2,1,0:T(8,128)(2,1)S(1)}, u32[]{:S(2)}, u32[]{:S(2)}) collective-permute-start(bf16[2,2,128,128]{3,2,1,0:T(8,128)(2,1)S(1)} %get-tuple-element.44), channel_id=1, source_target_pairs={{0,32},{4,36},{8,40},{12,44},{16,48},{20,52},{24,56},{28,60},{32,6... | collective-permute-start | bytes 393224 | tf_op jit(solution)/shard_map/ppermute | solution.py:561
  37.4 2.7 %collective-permute-start.6 = (bf16[2,2,128,128]{3,2,1,0:T(8,128)(2,1)S(1)}, bf16[2,2,128,128]{3,2,1,0:T(8,128)(2,1)S(1)}, u32[]{:S(2)}, u32[]{:S(2)}) collective-permute-start(bf16[2,2,128,128]{3,2,1,0:T(8,128)(2,1)S(1)} %get-tuple-element.45), channel_id=1, source_target_pairs={{0,64},{4,68},{8,72},{12,76},{16,80},{20,84},{24,88},{28,92},{32,9... | collective-permute-start | bytes 393224 | tf_op jit(solution)/shard_map/ppermute | solution.py:561
  40.1 1.4 %collective-permute-start.7 = (bf16[2,2,128,128]{3,2,1,0:T(8,128)(2,1)S(1)}, bf16[2,2,128,128]{3,2,1,0:T(8,128)(2,1)S(1)}, u32[]{:S(2)}, u32[]{:S(2)}) collective-permute-start(bf16[2,2,128,128]{3,2,1,0:T(8,128)(2,1)S(1)} %get-tuple-element.46), channel_id=1, source_target_pairs={{0,96},{4,100},{8,104},{12,108},{16,112},{20,116},{24,120},{28,124... | collective-permute-start | bytes 393224 | tf_op jit(solution)/shard_map/ppermute | solution.py:561
  41.6 1.0 collective-permute-done.5.one_ref
  42.5 3.8 %collective-permute-done.6.two_ref = bf16[2,2,128,128]{3,2,1,0:T(8,128)(2,1)S(1)} collective-permute-done((bf16[2,2,128,128]{3,2,1,0:T(8,128)(2,1)S(1)}, bf16[2,2,128,128]{3,2,1,0:T(8,128)(2,1)S(1)}, u32[]{:S(2)}, u32[]{:S(2)}) %collective-permute-start.6) | collective-permute-done | bytes 131104 | tf_op jit(solution)/shard_map/ppermute | solution.py:561
  46.3 6.0 %back.1 = (bf16[2,256,896]{2,1,0:T(8,128)(2,1)S(1)}, f32[16,128]{1,0:T(8,128)S(1)}) custom-call(s32[6]{0:T(128)S(1)} %stack.27.place_ref.core_ref, f32[4,3,256,128]{3,2,1,0:T(8,128)S(1)} %copy-done.10, f32[4,4,256,128]{3,2,1,0:T(8,128)S(1)} %extra.1.extra_ref, f32[4,256,128]{2,1,0:T(8,128)S(1)} %get-tuple-element.40.gates_ref, ...), custom_call_target="tpu_custom_call" | custom-call | flops 4000000000 | bytes 8000000 | tf_op jit(solution)/shard_map/back/pallas_call | solution.py:199
  52.4 1.8 %give.1 = (bf16[272,768]{1,0:T(8,128)(2,1)S(1)}, bf16[272,768]{1,0:T(8,128)(2,1)S(1)}, bf16[272,768]{1,0:T(8,128)(2,1)S(1)}, bf16[272,768]{1,0:T(8,128)(2,1)S(1)}, bf16[256,896]{1,0:T(8,128)(2,1)S(1)}) custom-call(s32[6]{0:T(128)S(1)} %stack.27.place_ref.core_ref, bf16[2,4,4,64,512]{4,3,2,1,0:T(8,128)(2,1)S(1)} %flip.1.after_ref.flipped_ref, ...), custom_call_target="tpu_custom_call" | custom-call | flops 1000000000 | bytes 4000000 | tf_op jit(solution)/shard_map/give/pallas_call | solution.py:376
  54.3 0.5 collective-permute-start.15
  54.8 1.0 %collective-permute-start.16 = (bf16[272,768]{1,0:T(8,128)(2,1)S(1)}, bf16[272,768]{1,0:T(8,128)(2,1)S(1)}, u32[]{:S(2)}, u32[]{:S(2)}) collective-permute-start(bf16[272,768]{1,0:T(8,128)(2,1)S(1)} %get-tuple-element.59), channel_id=1, source_target_pairs={{0,36},{4,8},{8,44},{12,16},{16,52},{20,24},{24,60},{28,0},{32,68}... | collective-permute-start | bytes 1253384 | tf_op jit(solution)/shard_map/ppermute | solution.py:611
  55.9 0.9 collective-permute-start.17
  56.8 1.2 %collective-permute-start.18 = (bf16[272,768]{1,0:T(8,128)(2,1)S(1)}, bf16[272,768]{1,0:T(8,128)(2,1)S(1)}, u32[]{:S(2)}, u32[]{:S(2)}) collective-permute-start(bf16[272,768]{1,0:T(8,128)(2,1)S(1)} %get-tuple-element.61), channel_id=1, source_target_pairs={{0,68},{4,16},{8,76},{12,24},{16,84},{20,0},{24,92},{28,8},{32,100... | collective-permute-start | bytes 1253384 | tf_op jit(solution)/shard_map/ppermute | solution.py:611
  58.0 1.8 %keep.1 = (bf16[272,768]{1,0:T(8,128)(2,1)S(1)}, bf16[272,768]{1,0:T(8,128)(2,1)S(1)}, bf16[272,768]{1,0:T(8,128)(2,1)S(1)}, bf16[272,768]{1,0:T(8,128)(2,1)S(1)}) custom-call(s32[6]{0:T(128)S(1)} %stack.27.place_ref.core_ref, bf16[2,4,4,64,512]{4,3,2,1,0:T(8,128)(2,1)S(1)} %flip.1.after_ref.flipped_ref, ...), custom_call_target="tpu_custom_call" | custom-call | flops 1000000000 | bytes 4000000 | tf_op jit(solution)/shard_map/keep/pallas_call | solution.py:376
  59.8 2.5 %collective-permute-start.13 = (bf16[272,768]{1,0:T(8,128)(2,1)S(1)}, bf16[272,768]{1,0:T(8,128)(2,1)S(1)}, u32[]{:S(2)}, u32[]{:S(2)}) collective-permute-start(bf16[272,768]{1,0:T(8,128)(2,1)S(1)} %get-tuple-element.56), channel_id=1, source_target_pairs={{0,24},{4,100},{8,0},{12,108},{16,8},{20,116},{24,16},{28,124},{32... | collective-permute-start | bytes 1253384 | tf_op jit(solution)/shard_map/ppermute | solution.py:561
  62.3 5.7 %collective-permute-done.16.refs_5_ = bf16[272,768]{1,0:T(8,128)(2,1)S(1)} collective-permute-done((bf16[272,768]{1,0:T(8,128)(2,1)S(1)}, bf16[272,768]{1,0:T(8,128)(2,1)S(1)}, u32[]{:S(2)}, u32[]{:S(2)}) %collective-permute-start.16) | collective-permute-done | bytes 417824 | tf_op jit(solution)/shard_map/ppermute | solution.py:611
  68.0 3.4 %inputs.1 = (bf16[256,512]{1,0:T(8,128)(2,1)S(1)}, bf16[256,512]{1,0:T(8,128)(2,1)S(1)}, bf16[256,512]{1,0:T(8,128)(2,1)S(1)}, bf16[256,512]{1,0:T(8,128)(2,1)S(1)}) custom-call(s32[6]{0:T(128)S(1)} %stack.27.place_ref.core_ref, bf16[2,256,896]{2,1,0:T(8,128)(2,1)S(1)} %get-tuple-element.47.grads_ref.mine_ref, ...), custom_call_target="tpu_custom_call" | custom-call | flops 40000000000 | bytes 8000000 | tf_op jit(solution)/shard_map/inputs/pallas_call | solution.py:624
  71.5 4.8 %collective-permute-done.13.refs_2_ = bf16[272,768]{1,0:T(8,128)(2,1)S(1)} collective-permute-done((bf16[272,768]{1,0:T(8,128)(2,1)S(1)}, bf16[272,768]{1,0:T(8,128)(2,1)S(1)}, u32[]{:S(2)}, u32[]{:S(2)}) %collective-permute-start.13) | collective-permute-done | bytes 417824 | tf_op jit(solution)/shard_map/ppermute | solution.py:561
  76.2 1.4 %collective-permute-done.14.refs_3_ = bf16[272,768]{1,0:T(8,128)(2,1)S(1)} collective-permute-done((bf16[272,768]{1,0:T(8,128)(2,1)S(1)}, bf16[272,768]{1,0:T(8,128)(2,1)S(1)}, u32[]{:S(2)}, u32[]{:S(2)}) %collective-permute-start.14) | collective-permute-done | bytes 417824 | tf_op jit(solution)/shard_map/ppermute | solution.py:561
  77.6 4.1 %collective-permute-done.12.refs_1_ = bf16[272,768]{1,0:T(8,128)(2,1)S(1)} collective-permute-done((bf16[272,768]{1,0:T(8,128)(2,1)S(1)}, bf16[272,768]{1,0:T(8,128)(2,1)S(1)}, u32[]{:S(2)}, u32[]{:S(2)}) %collective-permute-start.12) | collective-permute-done | bytes 417824 | tf_op jit(solution)/shard_map/ppermute | solution.py:561
  81.7 1.1 %middle.1 = (f32[2,80,768]{2,1,0:T(8,128)S(1)}, bf16[2,80,768]{2,1,0:T(8,128)(2,1)S(1)}, bf16[2,80,768]{2,1,0:T(8,128)(2,1)S(1)}, bf16[2,80,768]{2,1,0:T(8,128)(2,1)S(1)}) custom-call(s32[6]{0:T(128)S(1)} %stack.27.place_ref.core_ref, bf16[272,768]{1,0:T(8,128)(2,1)S(1)} %get-tuple-element.55.refs_0_, bf16[272,768]{1,0:T(8,128)(2,1)S(1)} %collective-permute-done.12.refs_1_, ...), custom_call_target="tpu_custom_call" | custom-call | tf_op jit(solution)/shard_map/middle/pallas_call | solution.py:453
  82.8 1.4 %collective-permute-start.19 = (bf16[2,80,768]{2,1,0:T(8,128)(2,1)S(1)}, bf16[2,80,768]{2,1,0:T(8,128)(2,1)S(1)}, u32[]{:S(2)}, u32[]{:S(2)}) collective-permute-start(bf16[2,80,768]{2,1,0:T(8,128)(2,1)S(1)} %get-tuple-element.63), channel_id=1, source_target_pairs={{0,32},{4,12},{8,40},{12,20},{16,48},{20,28},{24,56},{28,4},{32,64... | collective-permute-start | bytes 737288 | tf_op jit(solution)/shard_map/ppermute | solution.py:561
  84.2 1.9 %collective-permute-start.20 = (bf16[2,80,768]{2,1,0:T(8,128)(2,1)S(1)}, bf16[2,80,768]{2,1,0:T(8,128)(2,1)S(1)}, u32[]{:S(2)}, u32[]{:S(2)}) collective-permute-start(bf16[2,80,768]{2,1,0:T(8,128)(2,1)S(1)} %get-tuple-element.64), channel_id=1, source_target_pairs={{0,96},{4,28},{8,104},{12,4},{16,112},{20,12},{24,120},{28,20},{32... | collective-permute-start | bytes 737288 | tf_op jit(solution)/shard_map/ppermute | solution.py:561
  86.1 1.4 %collective-permute-start.21 = (bf16[2,80,768]{2,1,0:T(8,128)(2,1)S(1)}, bf16[2,80,768]{2,1,0:T(8,128)(2,1)S(1)}, u32[]{:S(2)}, u32[]{:S(2)}) collective-permute-start(bf16[2,80,768]{2,1,0:T(8,128)(2,1)S(1)} %get-tuple-element.65), channel_id=1, source_target_pairs={{0,64},{4,20},{8,72},{12,28},{16,80},{20,4},{24,88},{28,12},{32,96... | collective-permute-start | bytes 737288 | tf_op jit(solution)/shard_map/ppermute | solution.py:561
  87.5 1.9 %collective-permute-start.9 = (bf16[256,512]{1,0:T(8,128)(2,1)S(1)}, bf16[256,512]{1,0:T(8,128)(2,1)S(1)}, u32[]{:S(2)}, u32[]{:S(2)}) collective-permute-start(bf16[256,512]{1,0:T(8,128)(2,1)S(1)} %get-tuple-element.52), channel_id=1, source_target_pairs={{0,1},{1,2},{2,3},{3,0},{4,5},{5,6},{6,7},{7,4},{8,9},{9,10},{10,1... | collective-permute-start | bytes 786440 | tf_op jit(solution)/shard_map/ppermute | solution.py:646
  89.5 3.6 %collective-permute-start.10 = (bf16[256,512]{1,0:T(8,128)(2,1)S(1)}, bf16[256,512]{1,0:T(8,128)(2,1)S(1)}, u32[]{:S(2)}, u32[]{:S(2)}) collective-permute-start(bf16[256,512]{1,0:T(8,128)(2,1)S(1)} %get-tuple-element.53), channel_id=1, source_target_pairs={{0,2},{1,3},{2,0},{3,1},{4,6},{5,7},{6,4},{7,5},{8,10},{9,11},{10,... | collective-permute-start | bytes 786440 | tf_op jit(solution)/shard_map/ppermute | solution.py:646
  93.0 1.3 %collective-permute-start.11 = (bf16[256,512]{1,0:T(8,128)(2,1)S(1)}, bf16[256,512]{1,0:T(8,128)(2,1)S(1)}, u32[]{:S(2)}, u32[]{:S(2)}) collective-permute-start(bf16[256,512]{1,0:T(8,128)(2,1)S(1)} %get-tuple-element.54), channel_id=1, source_target_pairs={{0,3},{1,0},{2,1},{3,2},{4,7},{5,4},{6,5},{7,6},{8,11},{9,8},{10,9... | collective-permute-start | bytes 786440 | tf_op jit(solution)/shard_map/ppermute | solution.py:646
  94.3 1.3 %total.1 = (f32[64,512]{1,0:T(8,128)}, f32[64,512]{1,0:T(8,128)}, f32[64,512]{1,0:T(8,128)}, f32[16,128]{1,0:T(8,128)S(1)}) custom-call(s32[6]{0:T(128)S(1)} %stack.27.place_ref.core_ref, f32[2,80,768]{2,1,0:T(8,128)S(1)} %get-tuple-element.62.own_ref, bf16[2,80,768]{2,1,0:T(8,128)(2,1)S(1)} %collective-permute-done.19.one_ref, ...), custom_call_target="tpu_custom_call" | custom-call | tf_op jit(solution)/shard_map/total/pallas_call | solution.py:453
  95.6 0.6 slice_bitcast_fusion
  96.2 0.6 collective-permute-done.22
  96.8 0.6 fusion
  97.4 2.8 %collective-permute-done.10 = bf16[256,512]{1,0:T(8,128)(2,1)S(1)} collective-permute-done((bf16[256,512]{1,0:T(8,128)(2,1)S(1)}, bf16[256,512]{1,0:T(8,128)(2,1)S(1)}, u32[]{:S(2)}, u32[]{:S(2)}) %collective-permute-start.10) | collective-permute-done | bytes 262176 | tf_op jit(solution)/shard_map/ppermute | solution.py:646
  100.2 0.8 add_convert_fusion
  (37 shorter events, 0.3 us)
Async XLA Ops:
  0.6 7.6 %collective-permute-start = (bf16[256,2048]{1,0:T(8,128)(2,1)}, bf16[256,2048]{1,0:T(8,128)(2,1)S(1)}, u32[]{:S(2)}, u32[]{:S(2)}) collective-permute-start(bf16[256,2048]{1,0:T(8,128)(2,1)} %own_ref.1), channel_id=1, source_target_pairs={{0,4},{4,0},{8,12},{12,8},{16,20},{20,16},{24,28},{28,24},{32,36},... | collective-permute-start | bytes 3145736 | tf_op jit(solution)/shard_map/ppermute | solution.py:502
  0.7 7.5 %collective-permute-start.1 = (bf16[256,512]{1,0:T(8,128)(2,1)}, bf16[256,512]{1,0:T(8,128)(2,1)S(1)}, u32[]{:S(2)}, u32[]{:S(2)}) collective-permute-start(bf16[256,512]{1,0:T(8,128)(2,1)} %do_ref.5), channel_id=1, source_target_pairs={{0,4},{4,0},{8,12},{12,8},{16,20},{20,16},{24,28},{28,24},{32,36},... | collective-permute-start | bytes 786440 | tf_op jit(solution)/shard_map/ppermute | solution.py:502
  1.3 1.2 %copy-start = (bf16[256,2048]{1,0:T(8,128)(2,1)S(1)}, bf16[256,2048]{1,0:T(8,128)(2,1)}, u32[]{:S(2)}) copy-start(bf16[256,2048]{1,0:T(8,128)(2,1)} %own_ref.1) | copy-start | bytes 3145732
  2.5 1.6 %copy-start.2 = (bf16[2048,512]{1,0:T(8,128)(2,1)S(1)}, bf16[2048,512]{1,0:T(8,128)(2,1)}, u32[]{:S(2)}) copy-start(bf16[2048,512]{1,0:T(8,128)(2,1)} %wq_ref.5) | copy-start | bytes 6291460
  4.1 0.7 copy-start.6
  4.8 3.4 %copy-start.7 = (bf16[2048,4]{0,1:T(4,128)(2,1)S(1)}, bf16[2048,4]{0,1:T(4,128)(2,1)}, u32[]{:S(2)}) copy-start(bf16[2048,4]{0,1:T(4,128)(2,1)} %param.11) | copy-start | bytes 49156
  4.8 3.4 %copy-start.8 = (bf16[256,512]{1,0:T(8,128)(2,1)S(1)}, bf16[256,512]{1,0:T(8,128)(2,1)}, u32[]{:S(2)}) copy-start(bf16[256,512]{1,0:T(8,128)(2,1)} %do_ref.5) | copy-start | bytes 786436
  4.8 3.4 %copy-start.9 = (f32[4]{0:T(128)S(1)}, f32[4]{0:T(128)}, u32[]{:S(2)}) copy-start(f32[4]{0:T(128)} %bb_ref.1) | copy-start | bytes 52
  18.5 11.7 %collective-permute-start.4 = (bf16[2,3,128,128]{3,2,1,0:T(8,128)(2,1)S(1)}, bf16[2,3,128,128]{3,2,1,0:T(8,128)(2,1)S(1)}, u32[]{:S(2)}, u32[]{:S(2)}) collective-permute-start(bf16[2,3,128,128]{3,2,1,0:T(8,128)(2,1)S(1)} %get-tuple-element.42.after_ref.own_ref), channel_id=1, source_target_pairs={{0,24},{4,28},{8,0},{12,4},{16,8},{20,12},{24,16},{28,20},{32,56},... | collective-permute-start | bytes 589832 | tf_op jit(solution)/shard_map/ppermute | solution.py:561
  21.6 9.3 %collective-permute-start.3 = (bf16[2,3,128,128]{3,2,1,0:T(8,128)(2,1)S(1)}, bf16[2,3,128,128]{3,2,1,0:T(8,128)(2,1)S(1)}, u32[]{:S(2)}, u32[]{:S(2)}) collective-permute-start(bf16[2,3,128,128]{3,2,1,0:T(8,128)(2,1)S(1)} %get-tuple-element.42.after_ref.own_ref), channel_id=1, source_target_pairs={{0,16},{4,20},{8,24},{12,28},{16,0},{20,4},{24,8},{28,12},{32,48},... | collective-permute-start | bytes 589832 | tf_op jit(solution)/shard_map/ppermute | solution.py:561
  22.2 11.7 %collective-permute-start.2 = (bf16[2,3,128,128]{3,2,1,0:T(8,128)(2,1)S(1)}, bf16[2,3,128,128]{3,2,1,0:T(8,128)(2,1)S(1)}, u32[]{:S(2)}, u32[]{:S(2)}) collective-permute-start(bf16[2,3,128,128]{3,2,1,0:T(8,128)(2,1)S(1)} %get-tuple-element.42.after_ref.own_ref), channel_id=1, source_target_pairs={{0,8},{4,12},{8,16},{12,20},{16,24},{20,28},{24,0},{28,4},{32,40},... | collective-permute-start | bytes 589832 | tf_op jit(solution)/shard_map/ppermute | solution.py:561
  23.2 1.4 %copy-start.10 = (f32[4,3,256,128]{3,2,1,0:T(8,128)S(1)}, f32[4,3,256,128]{3,2,1,0:T(8,128)}, u32[]{:S(2)}) copy-start(f32[4,3,256,128]{3,2,1,0:T(8,128)} %get-tuple-element.38.saved_ref) | copy-start | bytes 4718596
  24.6 1.6 %copy-start.11 = (bf16[4,4,256,256]{3,2,1,0:T(8,128)(2,1)S(1)}, bf16[4,4,256,256]{3,2,1,0:T(8,128)(2,1)}, u32[]{:S(2)}) copy-start(bf16[4,4,256,256]{3,2,1,0:T(8,128)(2,1)} %get-tuple-element.39.solve_ref) | copy-start | bytes 6291460
  26.2 2.7 %copy-start.1 = (bf16[256,2048]{1,0:T(8,128)(2,1)S(1)}, bf16[256,2048]{1,0:T(8,128)(2,1)}, u32[]{:S(2)}) copy-start(bf16[256,2048]{1,0:T(8,128)(2,1)} %own_ref.1) | copy-start | bytes 3145732
  35.8 6.7 %collective-permute-start.5 = (bf16[2,2,128,128]{3,2,1,0:T(8,128)(2,1)S(1)}, bf16[2,2,128,128]{3,2,1,0:T(8,128)(2,1)S(1)}, u32[]{:S(2)}, u32[]{:S(2)}) collective-permute-start(bf16[2,2,128,128]{3,2,1,0:T(8,128)(2,1)S(1)} %get-tuple-element.44), channel_id=1, source_target_pairs={{0,32},{4,36},{8,40},{12,44},{16,48},{20,52},{24,56},{28,60},{32,6... | collective-permute-start | bytes 393224 | tf_op jit(solution)/shard_map/ppermute | solution.py:561
  37.4 8.9 %collective-permute-start.6 = (bf16[2,2,128,128]{3,2,1,0:T(8,128)(2,1)S(1)}, bf16[2,2,128,128]{3,2,1,0:T(8,128)(2,1)S(1)}, u32[]{:S(2)}, u32[]{:S(2)}) collective-permute-start(bf16[2,2,128,128]{3,2,1,0:T(8,128)(2,1)S(1)} %get-tuple-element.45), channel_id=1, source_target_pairs={{0,64},{4,68},{8,72},{12,76},{16,80},{20,84},{24,88},{28,92},{32,9... | collective-permute-start | bytes 393224 | tf_op jit(solution)/shard_map/ppermute | solution.py:561
  40.1 6.2 %collective-permute-start.7 = (bf16[2,2,128,128]{3,2,1,0:T(8,128)(2,1)S(1)}, bf16[2,2,128,128]{3,2,1,0:T(8,128)(2,1)S(1)}, u32[]{:S(2)}, u32[]{:S(2)}) collective-permute-start(bf16[2,2,128,128]{3,2,1,0:T(8,128)(2,1)S(1)} %get-tuple-element.46), channel_id=1, source_target_pairs={{0,96},{4,100},{8,104},{12,108},{16,112},{20,116},{24,120},{28,124... | collective-permute-start | bytes 393224 | tf_op jit(solution)/shard_map/ppermute | solution.py:561
  52.4 15.6 %copy-start.4 = (bf16[2048,512]{1,0:T(8,128)(2,1)S(1)}, bf16[2048,512]{1,0:T(8,128)(2,1)}, u32[]{:S(2)}) copy-start(bf16[2048,512]{1,0:T(8,128)(2,1)} %wk_ref.5) | copy-start | bytes 6291460
  52.4 15.6 %copy-start.5 = (bf16[2048,512]{1,0:T(8,128)(2,1)S(1)}, bf16[2048,512]{1,0:T(8,128)(2,1)}, u32[]{:S(2)}) copy-start(bf16[2048,512]{1,0:T(8,128)(2,1)} %wv_ref.5) | copy-start | bytes 6291460
  54.2 13.8 %copy-start.3 = (bf16[2048,512]{1,0:T(8,128)(2,1)S(1)}, bf16[2048,512]{1,0:T(8,128)(2,1)}, u32[]{:S(2)}) copy-start(bf16[2048,512]{1,0:T(8,128)(2,1)} %wq_ref.5) | copy-start | bytes 6291460
  54.2 13.8 %collective-permute-start.8 = (bf16[256,896]{1,0:T(8,128)(2,1)S(1)}, bf16[256,896]{1,0:T(8,128)(2,1)S(1)}, u32[]{:S(2)}, u32[]{:S(2)}) collective-permute-start(bf16[256,896]{1,0:T(8,128)(2,1)S(1)} %get-tuple-element.49), channel_id=1, source_target_pairs={{0,4},{4,0},{8,12},{12,8},{16,20},{20,16},{24,28},{28,24},{32,36},... | collective-permute-start | bytes 1376264 | tf_op jit(solution)/shard_map/ppermute | solution.py:502
  54.3 5.5 %collective-permute-start.15 = (bf16[272,768]{1,0:T(8,128)(2,1)S(1)}, bf16[272,768]{1,0:T(8,128)(2,1)S(1)}, u32[]{:S(2)}, u32[]{:S(2)}) collective-permute-start(bf16[272,768]{1,0:T(8,128)(2,1)S(1)} %get-tuple-element.58), channel_id=1, source_target_pairs={{0,4},{4,0},{8,12},{12,8},{16,20},{20,16},{24,28},{28,24},{32,36},... | collective-permute-start | bytes 1253384 | tf_op jit(solution)/shard_map/ppermute | solution.py:611
  54.8 13.2 %collective-permute-start.16 = (bf16[272,768]{1,0:T(8,128)(2,1)S(1)}, bf16[272,768]{1,0:T(8,128)(2,1)S(1)}, u32[]{:S(2)}, u32[]{:S(2)}) collective-permute-start(bf16[272,768]{1,0:T(8,128)(2,1)S(1)} %get-tuple-element.59), channel_id=1, source_target_pairs={{0,36},{4,8},{8,44},{12,16},{16,52},{20,24},{24,60},{28,0},{32,68}... | collective-permute-start | bytes 1253384 | tf_op jit(solution)/shard_map/ppermute | solution.py:611
  55.9 15.6 %collective-permute-start.17 = (bf16[272,768]{1,0:T(8,128)(2,1)S(1)}, bf16[272,768]{1,0:T(8,128)(2,1)S(1)}, u32[]{:S(2)}, u32[]{:S(2)}) collective-permute-start(bf16[272,768]{1,0:T(8,128)(2,1)S(1)} %get-tuple-element.60), channel_id=1, source_target_pairs={{0,100},{4,24},{8,108},{12,0},{16,116},{20,8},{24,124},{28,16},{32... | collective-permute-start | bytes 1253384 | tf_op jit(solution)/shard_map/ppermute | solution.py:611
  56.8 14.7 %collective-permute-start.18 = (bf16[272,768]{1,0:T(8,128)(2,1)S(1)}, bf16[272,768]{1,0:T(8,128)(2,1)S(1)}, u32[]{:S(2)}, u32[]{:S(2)}) collective-permute-start(bf16[272,768]{1,0:T(8,128)(2,1)S(1)} %get-tuple-element.61), channel_id=1, source_target_pairs={{0,68},{4,16},{8,76},{12,24},{16,84},{20,0},{24,92},{28,8},{32,100... | collective-permute-start | bytes 1253384 | tf_op jit(solution)/shard_map/ppermute | solution.py:611
  59.8 16.4 %collective-permute-start.13 = (bf16[272,768]{1,0:T(8,128)(2,1)S(1)}, bf16[272,768]{1,0:T(8,128)(2,1)S(1)}, u32[]{:S(2)}, u32[]{:S(2)}) collective-permute-start(bf16[272,768]{1,0:T(8,128)(2,1)S(1)} %get-tuple-element.56), channel_id=1, source_target_pairs={{0,24},{4,100},{8,0},{12,108},{16,8},{20,116},{24,16},{28,124},{32... | collective-permute-start | bytes 1253384 | tf_op jit(solution)/shard_map/ppermute | solution.py:561
  68.0 9.7 %collective-permute-start.14 = (bf16[272,768]{1,0:T(8,128)(2,1)S(1)}, bf16[272,768]{1,0:T(8,128)(2,1)S(1)}, u32[]{:S(2)}, u32[]{:S(2)}) collective-permute-start(bf16[272,768]{1,0:T(8,128)(2,1)S(1)} %get-tuple-element.57), channel_id=1, source_target_pairs={{0,16},{4,68},{8,24},{12,76},{16,0},{20,84},{24,8},{28,92},{32,48}... | collective-permute-start | bytes 1253384 | tf_op jit(solution)/shard_map/ppermute | solution.py:561
  68.0 13.7 %collective-permute-start.12 = (bf16[272,768]{1,0:T(8,128)(2,1)S(1)}, bf16[272,768]{1,0:T(8,128)(2,1)S(1)}, u32[]{:S(2)}, u32[]{:S(2)}) collective-permute-start(bf16[272,768]{1,0:T(8,128)(2,1)S(1)} %get-tuple-element.50.after_ref), channel_id=1, source_target_pairs={{0,8},{4,36},{8,16},{12,44},{16,24},{20,52},{24,0},{28,60},{32,40}... | collective-permute-start | bytes 1253384 | tf_op jit(solution)/shard_map/ppermute | solution.py:561
  82.8 10.3 %collective-permute-start.19 = (bf16[2,80,768]{2,1,0:T(8,128)(2,1)S(1)}, bf16[2,80,768]{2,1,0:T(8,128)(2,1)S(1)}, u32[]{:S(2)}, u32[]{:S(2)}) collective-permute-start(bf16[2,80,768]{2,1,0:T(8,128)(2,1)S(1)} %get-tuple-element.63), channel_id=1, source_target_pairs={{0,32},{4,12},{8,40},{12,20},{16,48},{20,28},{24,56},{28,4},{32,64... | collective-permute-start | bytes 737288 | tf_op jit(solution)/shard_map/ppermute | solution.py:561
  84.2 10.1 %collective-permute-start.20 = (bf16[2,80,768]{2,1,0:T(8,128)(2,1)S(1)}, bf16[2,80,768]{2,1,0:T(8,128)(2,1)S(1)}, u32[]{:S(2)}, u32[]{:S(2)}) collective-permute-start(bf16[2,80,768]{2,1,0:T(8,128)(2,1)S(1)} %get-tuple-element.64), channel_id=1, source_target_pairs={{0,96},{4,28},{8,104},{12,4},{16,112},{20,12},{24,120},{28,20},{32... | collective-permute-start | bytes 737288 | tf_op jit(solution)/shard_map/ppermute | solution.py:561
  86.1 8.2 %collective-permute-start.21 = (bf16[2,80,768]{2,1,0:T(8,128)(2,1)S(1)}, bf16[2,80,768]{2,1,0:T(8,128)(2,1)S(1)}, u32[]{:S(2)}, u32[]{:S(2)}) collective-permute-start(bf16[2,80,768]{2,1,0:T(8,128)(2,1)S(1)} %get-tuple-element.65), channel_id=1, source_target_pairs={{0,64},{4,20},{8,72},{12,28},{16,80},{20,4},{24,88},{28,12},{32,96... | collective-permute-start | bytes 737288 | tf_op jit(solution)/shard_map/ppermute | solution.py:561
  87.5 9.9 %collective-permute-start.9 = (bf16[256,512]{1,0:T(8,128)(2,1)S(1)}, bf16[256,512]{1,0:T(8,128)(2,1)S(1)}, u32[]{:S(2)}, u32[]{:S(2)}) collective-permute-start(bf16[256,512]{1,0:T(8,128)(2,1)S(1)} %get-tuple-element.52), channel_id=1, source_target_pairs={{0,1},{1,2},{2,3},{3,0},{4,5},{5,6},{6,7},{7,4},{8,9},{9,10},{10,1... | collective-permute-start | bytes 786440 | tf_op jit(solution)/shard_map/ppermute | solution.py:646
  89.5 10.7 %collective-permute-start.10 = (bf16[256,512]{1,0:T(8,128)(2,1)S(1)}, bf16[256,512]{1,0:T(8,128)(2,1)S(1)}, u32[]{:S(2)}, u32[]{:S(2)}) collective-permute-start(bf16[256,512]{1,0:T(8,128)(2,1)S(1)} %get-tuple-element.53), channel_id=1, source_target_pairs={{0,2},{1,3},{2,0},{3,1},{4,6},{5,7},{6,4},{7,5},{8,10},{9,11},{10,... | collective-permute-start | bytes 786440 | tf_op jit(solution)/shard_map/ppermute | solution.py:646
  93.0 7.2 %collective-permute-start.11 = (bf16[256,512]{1,0:T(8,128)(2,1)S(1)}, bf16[256,512]{1,0:T(8,128)(2,1)S(1)}, u32[]{:S(2)}, u32[]{:S(2)}) collective-permute-start(bf16[256,512]{1,0:T(8,128)(2,1)S(1)} %get-tuple-element.54), channel_id=1, source_target_pairs={{0,3},{1,0},{2,1},{3,2},{4,7},{5,4},{6,5},{7,6},{8,11},{9,8},{10,9... | collective-permute-start | bytes 786440 | tf_op jit(solution)/shard_map/ppermute | solution.py:646
  95.6 1.2 %collective-permute-start.22 = (f32[16,128]{1,0:T(8,128)S(1)}, f32[16,128]{1,0:T(8,128)S(1)}, u32[]{:S(2)}, u32[]{:S(2)}) collective-permute-start(f32[16,128]{1,0:T(8,128)S(1)} %get-tuple-element.69), channel_id=1, source_target_pairs={{0,4},{4,0},{8,12},{12,8},{16,20},{20,16},{24,28},{28,24},{32,36},... | collective-permute-start | bytes 24584 | tf_op jit(solution)/shard_map/ppermute | solution.py:502
where the time goes:
time: 101 us
  Pallas kernels  34.6 us (34%)
  starting transfers between devices  28.8 us (29%)
  waiting for transfers between devices  28.1 us (28%)
  local copies, waits for them, and re-layouts  7.23 us (7%)
  other arithmetic  1.47 us (1%)
    pallas_call x4, Pallas kernels, by_core(): pl.pallas_call(kernel, grid_spec=pltpu.PrefetchScalarGridSpec(num_scalar_...  22.3 us
    ppermute x12, waiting for transfers between devices, shift(): return lax.ppermute(block, 'seq', along(k, axis))  19.1 us
    ppermute x12, starting transfers between devices, shift(): return lax.ppermute(block, 'seq', along(k, axis))  17.7 us
    ppermute x3, starting transfers between devices, per_device(): lax.ppermute(shifted[k], 'head', [(i, (i + k) % ring) for i in range(ring)])  6.76 us
    unnamed x24, local copies, waits for them, and re-layouts  6.57 us
    ppermute x4, waiting for transfers between devices, per_device(): given = [lax.ppermute(give[k], 'seq', across(k)) for k in (0, 1, 3, 2)]  5.67 us
    pallas_call x3, Pallas kernels, call(): pl.pallas_call(kernel, grid_spec=pltpu.PrefetchScalarGridSpec(num_scalar_...  4.28 us
    ppermute x4, starting transfers between devices, per_device(): given = [lax.ppermute(give[k], 'seq', across(k)) for k in (0, 1, 3, 2)]  3.66 us
  transfers between devices with their start and end apart: 23, of which 11 were waited for; matrix products, arithmetic and copies ran while one was open for 1% of the time, Pallas kernels for 13%

commit v1 on v0

--- a/solution.py
+++ b/solution.py
@@ -16,6 +16,7 @@
 FULL = PACK + WIDTH
 VMEM = 24 * 2**20
 BIG = 50 * 2**20
+CHUNK = 48
 SLAB = 16
 f32 = jnp.float32
 bf16 = jnp.bfloat16
@@ -279,6 +280,8 @@
     rank = lax.broadcasted_iota(jnp.int32, (SLAB, WIDTH), 0)
     shares = [jnp.zeros((ROWS, WIDTH), f32) for _ in range(2)]
     sums = jnp.zeros((SLAB, WIDTH), f32)
+    states, duals = [None] * 4, [None] * 4
+    starts, laters = [], []
     for head in range(2):
         start = jnp.zeros((WIDTH, WIDTH), f32)
         later = jnp.zeros((WIDTH, WIDTH), f32)
@@ -287,62 +290,71 @@
             if k < 3:
                 moved = moved - dot(start, (rows_of[k][head, 0], None))
             start = jnp.where(x >= k, moved, start)
-        for k in (1, 2, 3):
-            moved = later + rows_of[k][head, 1].astype(f32)
-            if k > 1:
-                moved = moved - dot(later, (rows_of[k][head, 0], None), NT)
-            later = jnp.where(x < k, moved, later)
-        start = start + span_ref[head, 1] - dot(start, span_ref[head, 0])
-        later = later + span_ref[head, 3] - dot(later, span_ref[head, 2], NT)
+            m = SIDE - k
+            moved = later + rows_of[m][head, 1].astype(f32)
+            if m > 1:
+                moved = moved - dot(later, (rows_of[m][head, 0], None), NT)
+            later = jnp.where(x < m, moved, later)
+        starts.append(start)
+        laters.append(later)
+    starts = [s + span_ref[h, 1] - dot(s, span_ref[h, 0]) for h, s in enumerate(starts)]
+    laters = [s + span_ref[h, 3] - dot(s, span_ref[h, 2], NT) for h, s in enumerate(laters)]
+    for head in range(2):
         mine = [maps_ref[head, i] for i in range(3)]
         theirs = [maps_ref[2 + head, i] for i in range(3)]
         d1, o1 = (jnp.where(early, mine[i], theirs[i]) for i in (0, 1))
         d2, a2 = (jnp.where(early, theirs[i], mine[i]) for i in (0, 2))
+        start, later = starts[head], laters[head]
         middle = start + o1 - dot(start, d1)
         inner = later + a2 - dot(later, d2, NT)
-        states = (jnp.where(early, start, middle), jnp.where(early, middle, start))
-        duals = (jnp.where(early, inner, later), jnp.where(early, later, inner))
-        for unit in range(2):
-            case = 2 * unit + head
-            d_out = (do_ref, sdo_ref)[unit][:, head * WIDTH : (head + 1) * WIDTH]
-            qn, kn = saved_ref[case, 0], saved_ref[case, 1]
-            gates = gates_ref[case]
-            beta, rq, rk = gates[:, 0:1], gates[:, 1:2], gates[:, 2:3]
-            state, dual = split(states[unit]), split(duals[unit])
-            error = extra_ref[case, 1] - dot(extra_ref[case, 0], state, NT)
-            y = extra_ref[case, 3] + dot(extra_ref[case, 2], dual, NT)
-            update = split(beta * error)
-            dv = beta * y
-            dvb = dv.astype(bf16)
-            ks, qs = split(kn), split(qn)
-            pulls = jnp.concatenate([d_out, dvb], 0)
-            products = dot((pulls, None), update, NT)
-            dm = jnp.where(row >= col, products[:ROWS], 0.0).astype(bf16)
-            dn = jnp.where(row > col, products[ROWS:], 0.0).astype(bf16)
-            lefts = dot((jnp.concatenate([dm, dn], 0), None), ks)
-            rights = dot((pulls, None), state)
-            both = tuple(jnp.concatenate([a, b], 0) for a, b in zip(qs, ks))
-            dqn = rights[:ROWS] + lefts[:ROWS]
-            dkn = (
-                dot((jnp.concatenate([dm, -dn], 0), None), both, TN)
-                + dot((update[0], None), dual)
-                - lefts[ROWS:]
-                - rights[ROWS:]
-            )
-            dq = rq * (dqn - qn * jnp.sum(qn * dqn, 1, keepdims=True))
-            dk = rk * (dkn - kn * jnp.sum(kn * dkn, 1, keepdims=True))
-            dz = jnp.sum(y * error, 1, keepdims=True) * beta * (1.0 - 0.5 * beta)
-            for place, grad in enumerate((dq, dk, dv)):
-                base = place * PAIR + head * WIDTH
-                grads_ref[unit, :, base : base + WIDTH] = grad.astype(bf16)
-            shares[unit] = shares[unit] + jnp.where(lane == 2 * core + head, dz, 0.0)
-            sums = sums + jnp.where(rank == 4 + 2 * core + head, jnp.sum(dz, 0, keepdims=True), 0.0)
+        states[head] = split(jnp.where(early, start, middle))
+        states[2 + head] = split(jnp.where(early, middle, start))
+        duals[head] = split(jnp.where(early, inner, later))
+        duals[2 + head] = split(jnp.where(early, later, inner))
+    every = range(4)
+    cuts = [slice((i % 2) * WIDTH, (i % 2 + 1) * WIDTH) for i in every]
+    qns = [saved_ref[i, 0] for i in every]
+    kns = [saved_ref[i, 1] for i in every]
+    betas = [gates_ref[i, :, 0:1] for i in every]
+    errors = [extra_ref[i, 1] - dot(extra_ref[i, 0], states[i], NT) for i in every]
+    ys = [extra_ref[i, 3] + dot(extra_ref[i, 2], duals[i], NT) for i in every]
+    updates = [split(b * e) for b, e in zip(betas, errors)]
+    dvs = [(b * y).astype(bf16) for b, y in zip(betas, ys)]
+    pulls = [
+        (jnp.concatenate([(do_ref, sdo_ref)[i // 2][:, cuts[i]], dvs[i]], 0), None) for i in every
+    ]
+    products = [dot(p, u, NT) for p, u in zip(pulls, updates)]
+    dms = [jnp.where(row >= col, p[:ROWS], 0.0).astype(bf16) for p in products]
+    dns = [jnp.where(row > col, p[ROWS:], 0.0).astype(bf16) for p in products]
+    qs, ks = [split(q) for q in qns], [split(k) for k in kns]
+    lefts = [dot((jnp.concatenate([m, n], 0), None), k) for m, n, k in zip(dms, dns, ks)]
+    rights = [dot(p, s) for p, s in zip(pulls, states)]
+    both = [
+        tuple(jnp.concatenate([a, b], 0) for a, b in zip(q, k)) for q, k in zip(qs, ks)
+    ]
+    turned = [
+        dot((jnp.concatenate([m, -n], 0), None), t, TN) for m, n, t in zip(dms, dns, both)
+    ]
+    carried = [dot((u[0], None), d) for u, d in zip(updates, duals)]
+    for i in every:
+        unit, head = i // 2, i % 2
+        dqn = rights[i][:ROWS] + lefts[i][:ROWS]
+        dkn = turned[i] + carried[i] - lefts[i][ROWS:] - rights[i][ROWS:]
+        qn, kn, beta = qns[i], kns[i], betas[i]
+        dq = gates_ref[i, :, 1:2] * (dqn - qn * jnp.sum(qn * dqn, 1, keepdims=True))
+        dk = gates_ref[i, :, 2:3] * (dkn - kn * jnp.sum(kn * dkn, 1, keepdims=True))
+        dz = jnp.sum(ys[i] * errors[i], 1, keepdims=True) * beta * (1.0 - 0.5 * beta)
+        for place, grad in enumerate((dq.astype(bf16), dk.astype(bf16), dvs[i])):
+            base = place * PAIR + head * WIDTH
+            grads_ref[unit, :, base : base + WIDTH] = grad
+        shares[unit] = shares[unit] + jnp.where(lane == 2 * core + head, dz, 0.0)
+        sums = sums + jnp.where(rank == 4 + 2 * core + head, jnp.sum(dz, 0, keepdims=True), 0.0)
     for unit in range(2):
         grads_ref[unit, :, PACK:] = shares[unit].astype(bf16)
     sums_ref[...] = sums
 
 
-def weights_kernel(away, place_ref, flipped_ref, grads_ref, sums_ref, *outs):
+def weights_kernel(away, place_ref, flipped_ref, grads_ref, sums_ref, after_ref, *outs):
     rows = flipped_ref.shape[3]
     span = SIDE * rows
     grads = grads_ref[:, :, :PACK].reshape(2 * ROWS, PACK)
@@ -357,18 +369,31 @@
     for k in range(SIDE):
         cut = slice(k * span, (k + 1) * span)
         outs[k][:span] = total[cut]
-        outs[k][span:, :span] = high[:, cut]
-        outs[k][span:, span : 2 * span] = low[:, cut]
-        outs[k][span:, 2 * span :] = jnp.zeros((SLAB, PACK - 2 * span), bf16)
+        last = span + SLAB
+        outs[k][span:last, :span] = high[:, cut]
+        outs[k][span:last, span : 2 * span] = low[:, cut]
+        outs[k][span:last, 2 * span :] = jnp.zeros((SLAB, PACK - 2 * span), bf16)
     if away:
-        outs[SIDE][...] = grads_ref[1]
-
-
-def weights_pass(name, away, place, flipped, grads, sums):
+        base = span + SLAB
+        outs[0][base : base + ROWS] = grads_ref[1, :, :PACK]
+        base = base + ROWS
+        for tile in range(PACK // WIDTH):
+            count = min(CHUNK, ROWS - tile * CHUNK)
+            column = slice(tile * WIDTH, (tile + 1) * WIDTH)
+            outs[0][base : base + count, column] = grads_ref[
+                1, tile * CHUNK : tile * CHUNK + count, PACK:
+            ]
+            if count < CHUNK:
+                outs[0][base + count : base + CHUNK, column] = jnp.zeros(
+                    (CHUNK - count, WIDTH), bf16
+                )
+
+
+def weights_pass(name, away, place, flipped, grads, sums, after):
     rows = flipped.shape[3]
     shapes = [jax.ShapeDtypeStruct((SIDE * rows + SLAB, PACK), bf16)] * SIDE
     if away:
-        shapes.append(jax.ShapeDtypeStruct(grads.shape[1:], bf16))
+        shapes[0] = jax.ShapeDtypeStruct((SIDE * rows + SLAB + ROWS + CHUNK, PACK), bf16)
 
     def whole(shape):
         return pl.BlockSpec(shape, lambda k, p: (0,) * len(shape))
@@ -385,6 +410,7 @@
                 ),
                 whole(grads.shape),
                 whole(sums.shape),
+                pl.BlockSpec(memory_space=pl.ANY),
             ],
             out_specs=[whole(s.shape) for s in shapes],
         ),
@@ -392,7 +418,7 @@
         compiler_params=pltpu.CompilerParams(vmem_limit_bytes=VMEM),
         cost_estimate=pl.CostEstimate(flops=10**9, bytes_accessed=4 * 10**6, transcendentals=0),
         name=name,
-    )(place, flipped, grads, sums)
+    )(place, flipped, grads, sums, after)
 
 
 def fair_sum(terms):
@@ -407,7 +433,11 @@
     for pair in range(2):
         group = inputs[pair * SIDE : (pair + 1) * SIDE]
         slab = fair_sum(
-            [ref[span:, :span].astype(f32) + ref[span:, span : 2 * span].astype(f32) for ref in group]
+            [
+                ref[span : span + SLAB, :span].astype(f32)
+                + ref[span : span + SLAB, span : 2 * span].astype(f32)
+                for ref in group
+            ]
         )
         for k in range(SIDE):
             slot = lax.rem(base + k, SIDE)
@@ -424,7 +454,7 @@
             outs[k][pair, rows:, 2 * WIDTH :] = jnp.zeros((SLAB, PACK - 2 * WIDTH), kind)
 
 
-def total_kernel(core_ref, own_ref, one_ref, two_ref, three_ref, *outs):
+def total_kernel(core_ref, own_ref, one_ref, two_ref, three_ref, after_ref, *outs):
     early = core_ref[0] == 0
     rows = own_ref.shape[1] - SLAB
     sums = []
@@ -437,7 +467,9 @@
         sums.append(total)
         slabs = [ref[pair, rows:, : 2 * WIDTH].astype(f32) for ref in refs]
         tails.append(fair_sum([t[:, :WIDTH] + t[:, WIDTH:] for t in slabs]))
-    outs[3][...] = tails[0] + tails[1]
+    tail = tails[0] + tails[1]
+    outs[3][...] = tail[: outs[3].shape[0], :rows]
+    outs[4][...] = tail
     low = jnp.where(early, sums[0], sums[1])
     high = jnp.where(early, sums[1], sums[0])
     for place, out in enumerate(outs[:3]):
@@ -471,12 +503,18 @@
     core, step = place_ref[0], pl.program_id(0)
     near = pl.ds(pl.multiple_of(core * PAIR, PAIR), PAIR)
     far = pl.ds(pl.multiple_of((1 - core) * PAIR, PAIR), PAIR)
-    shares = (mine_ref[0, :, PACK:] + other_ref[:, PACK:])[:, : wb_ref.shape[0]]
-    total = one(shares, wb_ref[...], NN)
+    base = other_ref.shape[0] - CHUNK
+    tiles = [
+        other_ref[base : base + min(CHUNK, ROWS - t * CHUNK), t * WIDTH : (t + 1) * WIDTH]
+        for t in range(PACK // WIDTH)
+    ]
+    shares = mine_ref[0, :, PACK:] + jnp.concatenate(tiles, 0)
+    total = one(shares[:, : wb_ref.shape[0]], wb_ref[...], NN)
+    base = base - ROWS
     for place, w_ref in enumerate((wq_ref, wk_ref, wv_ref)):
         cut = slice(place * PAIR, (place + 1) * PAIR)
         total = total + one(mine_ref[0, :, cut], w_ref[:, near], NT)
-        total = total + one(other_ref[:, cut], w_ref[:, far], NT)
+        total = total + one(other_ref[base : base + ROWS, cut], w_ref[:, far], NT)
     total = total.astype(bf16)
     for k, out in enumerate(outs):
 
@@ -514,7 +552,7 @@
         [jax.ShapeDtypeStruct((ROWS, PACK + WIDTH), f32)],
         10**9,
         5 * 10**6,
-        BIG,
+        60 * 2**20,
     )
     saved, solved, gates, own_maps, send = by_core(
         local_kernel,
@@ -607,10 +645,9 @@
     def across(k):
         return [(i, j ^ 1) for i, j in along(k, lambda c: c == 0)]
 
-    *give, relay = weights_pass("give", 1, place, flipped, grads, sums)
+    give = weights_pass("give", 1, place, flipped, grads, sums, sums)
     given = [lax.ppermute(give[k], "seq", across(k)) for k in (0, 1, 3, 2)]
-    other_grads = swap(relay)
-    keep = weights_pass("keep", 0, place, flipped, grads, sums)
+    keep = weights_pass("keep", 0, place, flipped, grads, sums, given[0])
     kept = [keep[0]] + [shift(keep[k], k, lambda c: c == 1) for k in (1, 3, 2)]
 
     width = depth // ring
@@ -626,7 +663,7 @@
         grid_spec=pltpu.PrefetchScalarGridSpec(
             num_scalar_prefetch=1,
             grid=(ring,),
-            in_specs=[full((1, ROWS, FULL)), full((ROWS, FULL))]
+            in_specs=[full((1, ROWS, FULL)), full(given[0].shape)]
             + [rows_at(w_query.shape[1])] * 3
             + [
                 pl.BlockSpec((wb.shape[0], width), lambda i, p: (0, lax.rem(i + p[3], ring))),
@@ -640,7 +677,7 @@
             flops=4 * 10**10, bytes_accessed=8 * 10**6, transcendentals=0
         ),
         name="inputs",
-    )(place, grads, other_grads, w_query, w_key, w_value, wb, keep[1])
+    )(place, grads, given[0], w_query, w_key, w_value, wb, keep[1])
 
     arrived = [
         lax.ppermute(shifted[k], "head", [(i, (i + k) % ring) for i in range(ring)])
@@ -662,17 +699,21 @@
         idle=[shifted[0]],
     )
     final = [shift(passed[k], k, lambda c: c == 0) for k in (1, 3, 2)]
-    grad_query, grad_key, grad_value, tail = call(
+    heads = w_beta.shape[1]
+    grad_query, grad_key, grad_value, grad_wbeta, tail = call(
         "total",
         total_kernel,
         place,
         [passed[0], *final],
         [jax.ShapeDtypeStruct((rows, 2 * PAIR), f32)] * 3
-        + [jax.ShapeDtypeStruct((SLAB, WIDTH), f32)],
-    )
-    heads = w_beta.shape[1]
+        + [
+            jax.ShapeDtypeStruct((heads, rows), f32),
+            jax.ShapeDtypeStruct((SLAB, WIDTH), f32),
+        ],
+        idle=[d_x],
+    )
     grad_bbeta = jnp.where(core == 0, tail, swap(tail))[4 : 4 + heads, 0]
-    return (d_x, grad_query, grad_key, grad_value, tail[:heads, :rows].T, grad_bbeta)
+    return (d_x, grad_query, grad_key, grad_value, grad_wbeta.T, grad_bbeta)
 
 
 def solution(mesh):

time: 101 us -> 97 us (0.960); the launches traced: 101 us -> 95.6 us
  waiting for transfers between devices: 28.1 us -> 24.3 us
  local copies, waits for them, and re-layouts: 7.23 us -> 4.89 us
  starting transfers between devices: 28.8 us -> 30.2 us
    ppermute x12, waiting for transfers between devices: 19.1 us -> 13.7 us  [shift(): return lax.ppermute(block, 'seq', along(k, axis))]
    ppermute x4, waiting for transfers between devices: 5.67 us -> 8.2 us  [per_device(): given = [lax.ppermute(give[k], 'seq', across(k)) for k in (0, 1, 3, 2)]]
    unnamed x24 -> x26, local copies, waits for them, and re-layouts: 6.57 us -> 4.22 us
    ppermute x12, starting transfers between devices: 17.7 us -> 19.3 us  [shift(): return lax.ppermute(block, 'seq', along(k, axis))]
    ppermute x3, waiting for transfers between devices: 2.76 us -> 1.21 us  [per_device(): lax.ppermute(shifted[k], 'head', [(i, (i + k) % ring) for i in range(ring)])]
  transfers between devices with their start and end apart: 23 -> 22, of which waited for: 11 -> 12; matrix products, arithmetic and copies ran while one was open for 1% -> 1% of each run, Pallas kernels for 13% -> 16%
where the time goes in v1:
time: 97 us; the launch traced here: 95.6 us
  Pallas kernels  34.6 us (36%)
  starting transfers between devices  30.2 us (31%)
  waiting for transfers between devices  24.3 us (25%)
  local copies, waits for them, and re-layouts  4.89 us (5%)
    pallas_call x4, Pallas kernels, by_core(): pl.pallas_call(kernel, grid_spec=pltpu.PrefetchScalarGridSpec(num_scalar_...  22.4 us
    ppermute x12, starting transfers between devices, shift(): return lax.ppermute(block, 'seq', along(k, axis))  19.3 us
    ppermute x12, waiting for transfers between devices, shift(): return lax.ppermute(block, 'seq', along(k, axis))  13.7 us
    ppermute x4, waiting for transfers between devices, per_device(): given = [lax.ppermute(give[k], 'seq', across(k)) for k in (0, 1, 3, 2)]  8.2 us
    ppermute x3, starting transfers between devices, per_device(): lax.ppermute(shifted[k], 'head', [(i, (i + k) % ring) for i in range(ring)])  6.59 us
    pallas_call x3, Pallas kernels, call(): pl.pallas_call(kernel, grid_spec=pltpu.PrefetchScalarGridSpec(num_scalar_...  4.28 us
    unnamed x26, local copies, waits for them, and re-layouts  4.22 us
    ppermute x4, starting transfers between devices, per_device(): given = [lax.ppermute(give[k], 'seq', across(k)) for k in (0, 1, 3, 2)]  3.64 us
  transfers between devices with their start and end apart: 22, of which 12 were waited for; matrix products, arithmetic and copies ran while one was open for 1% of the time, Pallas kernels for 16%

profile of v1, /device:TPU:0, one launch (start us, length us, event | category | flops | bytes accessed | tf_op | source)
XLA Modules:
  0.0 95.6 jit_solution(12837867494429902148)
XLA Ops:
  0.6 0.1 collective-permute-start
  0.7 0.5 collective-permute-start.1
  1.2 0.7 stack.27.place_ref.core_ref
  1.9 5.2 %project.1.own_ref = f32[256,896]{1,0:T(8,128)} custom-call(s32[6]{0:T(128)} %stack.27.place_ref.core_ref, bf16[256,2048]{1,0:T(8,128)(2,1)} %own_ref.1, bf16[2048,512]{1,0:T(8,128)(2,1)} %wq_ref.5, bf16[2048,512]{1,0:T(8,128)(2,1)} %wk_ref.5, bf16[2048,512]{1,0:T(8,128)(2,1)} %wv_ref.5, bf16[4,2048]{1,0:T(4,128)(2,1)} %bitcast.8), custom_call_target="tpu_custom_call" | custom-call | flops 1000000000 | bytes 5000000 | tf_op jit(solution)/shard_map/project/pallas_call | solution.py:200
  7.1 1.2 %copy-done.5 = f32[256,896]{1,0:T(8,128)S(1)} copy-done((f32[256,896]{1,0:T(8,128)S(1)}, f32[256,896]{1,0:T(8,128)}, u32[]{:S(2)}) %copy-start.5) | copy-done | bytes 917528
  8.3 10.2 %local.1 = (f32[4,3,256,128]{3,2,1,0:T(8,128)}, bf16[4,4,256,256]{3,2,1,0:T(8,128)(2,1)}, f32[4,256,128]{2,1,0:T(8,128)S(1)}, f32[4,3,128,128]{3,2,1,0:T(8,128)S(1)}, bf16[2,3,128,128]{3,2,1,0:T(8,128)(2,1)S(1)}) custom-call(s32[6]{0:T(128)S(1)} %copy-done.6, f32[256,896]{1,0:T(8,128)S(1)} %copy-done.5, ...), custom_call_target="tpu_custom_call" | custom-call | flops 10000000000 | bytes 10000000 | tf_op jit(solution)/shard_map/local/pallas_call | solution.py:200
  18.5 3.1 %collective-permute-start.4 = (bf16[2,3,128,128]{3,2,1,0:T(8,128)(2,1)S(1)}, bf16[2,3,128,128]{3,2,1,0:T(8,128)(2,1)S(1)}, u32[]{:S(2)}, u32[]{:S(2)}) collective-permute-start(bf16[2,3,128,128]{3,2,1,0:T(8,128)(2,1)S(1)} %get-tuple-element.42.after_ref.own_ref), channel_id=1, source_target_pairs={{0,24},{4,28},{8,0},{12,4},{16,8},{20,12},{24,16},{28,20},{32,56},... | collective-permute-start | bytes 589832 | tf_op jit(solution)/shard_map/ppermute | solution.py:599
  21.6 0.6 collective-permute-start.3
  22.2 1.0 %collective-permute-start.2 = (bf16[2,3,128,128]{3,2,1,0:T(8,128)(2,1)S(1)}, bf16[2,3,128,128]{3,2,1,0:T(8,128)(2,1)S(1)}, u32[]{:S(2)}, u32[]{:S(2)}) collective-permute-start(bf16[2,3,128,128]{3,2,1,0:T(8,128)(2,1)S(1)} %get-tuple-element.42.after_ref.own_ref), channel_id=1, source_target_pairs={{0,8},{4,12},{8,16},{12,20},{16,24},{20,28},{24,0},{28,4},{32,40},... | collective-permute-start | bytes 589832 | tf_op jit(solution)/shard_map/ppermute | solution.py:599
  23.2 1.4 %copy-done.10 = f32[4,3,256,128]{3,2,1,0:T(8,128)S(1)} copy-done((f32[4,3,256,128]{3,2,1,0:T(8,128)S(1)}, f32[4,3,256,128]{3,2,1,0:T(8,128)}, u32[]{:S(2)}) %copy-start.10) | copy-done | bytes 1572888
  24.6 1.6 %copy-done.12 = bf16[4,4,256,256]{3,2,1,0:T(8,128)(2,1)S(1)} copy-done((bf16[4,4,256,256]{3,2,1,0:T(8,128)(2,1)S(1)}, bf16[4,4,256,256]{3,2,1,0:T(8,128)(2,1)}, u32[]{:S(2)}) %copy-start.12) | copy-done | bytes 2097176
  26.2 2.7 %extra.1.extra_ref = f32[4,4,256,128]{3,2,1,0:T(8,128)S(1)} custom-call(s32[6]{0:T(128)S(1)} %copy-done.6, f32[4,3,256,128]{3,2,1,0:T(8,128)S(1)} %copy-done.10, bf16[4,4,256,256]{3,2,1,0:T(8,128)(2,1)S(1)} %copy-done.12, bf16[256,512]{1,0:T(8,128)(2,1)S(1)} %copy-done.8, bf16[256,512]{1,0:T(8,128)(2,1)S(1)} %collective-permute-done.1.sdo_ref), custom_call_target="tpu_custom_call" | custom-call | flops 10000000000 | bytes 5000000 | tf_op jit(solution)/shard_map/extra/pallas_call | solution.py:200
  28.9 1.0 %flip.1.after_ref.flipped_ref = bf16[2,4,4,64,512]{4,3,2,1,0:T(8,128)(2,1)S(1)} custom-call(bf16[256,2048]{1,0:T(8,128)(2,1)S(1)} %copy-done, bf16[256,2048]{1,0:T(8,128)(2,1)S(1)} %collective-permute-done.x_ref.sib_ref, bf16[2,3,128,128]{3,2,1,0:T(8,128)(2,1)S(1)} %get-tuple-element.42.after_ref.own_ref), custom_call_target="tpu_custom_call" | custom-call | bytes 8000000 | tf_op jit(solution)/shard_map/flip/pallas_call | solution.py:604
  29.9 0.3 collective-permute-done.4.three_ref
  30.2 0.7 collective-permute-done.3.two_ref
  30.9 3.0 %collective-permute-done.2.one_ref = bf16[2,3,128,128]{3,2,1,0:T(8,128)(2,1)S(1)} collective-permute-done((bf16[2,3,128,128]{3,2,1,0:T(8,128)(2,1)S(1)}, bf16[2,3,128,128]{3,2,1,0:T(8,128)(2,1)S(1)}, u32[]{:S(2)}, u32[]{:S(2)}) %collective-permute-start.2) | collective-permute-done | bytes 196640 | tf_op jit(solution)/shard_map/ppermute | solution.py:599
  33.9 1.9 %compose.1 = (f32[2,4,128,128]{3,2,1,0:T(8,128)S(1)}, bf16[2,2,128,128]{3,2,1,0:T(8,128)(2,1)S(1)}, bf16[2,2,128,128]{3,2,1,0:T(8,128)(2,1)S(1)}, bf16[2,2,128,128]{3,2,1,0:T(8,128)(2,1)S(1)}) custom-call(s32[6]{0:T(128)S(1)} %copy-done.6, bf16[2,3,128,128]{3,2,1,0:T(8,128)(2,1)S(1)} %get-tuple-element.42.after_ref.own_ref, ...), custom_call_target="tpu_custom_call" | custom-call | flops 1000000000 | tf_op jit(solution)/shard_map/compose/pallas_call | solution.py:485
  35.8 1.6 %collective-permute-start.5 = (bf16[2,2,128,128]{3,2,1,0:T(8,128)(2,1)S(1)}, bf16[2,2,128,128]{3,2,1,0:T(8,128)(2,1)S(1)}, u32[]{:S(2)}, u32[]{:S(2)}) collective-permute-start(bf16[2,2,128,128]{3,2,1,0:T(8,128)(2,1)S(1)} %get-tuple-element.44), channel_id=1, source_target_pairs={{0,32},{4,36},{8,40},{12,44},{16,48},{20,52},{24,56},{28,60},{32,6... | collective-permute-start | bytes 393224 | tf_op jit(solution)/shard_map/ppermute | solution.py:599
  37.4 2.7 %collective-permute-start.6 = (bf16[2,2,128,128]{3,2,1,0:T(8,128)(2,1)S(1)}, bf16[2,2,128,128]{3,2,1,0:T(8,128)(2,1)S(1)}, u32[]{:S(2)}, u32[]{:S(2)}) collective-permute-start(bf16[2,2,128,128]{3,2,1,0:T(8,128)(2,1)S(1)} %get-tuple-element.45), channel_id=1, source_target_pairs={{0,64},{4,68},{8,72},{12,76},{16,80},{20,84},{24,88},{28,92},{32,9... | collective-permute-start | bytes 393224 | tf_op jit(solution)/shard_map/ppermute | solution.py:599
  40.1 1.4 %collective-permute-start.7 = (bf16[2,2,128,128]{3,2,1,0:T(8,128)(2,1)S(1)}, bf16[2,2,128,128]{3,2,1,0:T(8,128)(2,1)S(1)}, u32[]{:S(2)}, u32[]{:S(2)}) collective-permute-start(bf16[2,2,128,128]{3,2,1,0:T(8,128)(2,1)S(1)} %get-tuple-element.46), channel_id=1, source_target_pairs={{0,96},{4,100},{8,104},{12,108},{16,112},{20,116},{24,120},{28,124... | collective-permute-start | bytes 393224 | tf_op jit(solution)/shard_map/ppermute | solution.py:599
  41.5 1.0 %collective-permute-done.5.one_ref = bf16[2,2,128,128]{3,2,1,0:T(8,128)(2,1)S(1)} collective-permute-done((bf16[2,2,128,128]{3,2,1,0:T(8,128)(2,1)S(1)}, bf16[2,2,128,128]{3,2,1,0:T(8,128)(2,1)S(1)}, u32[]{:S(2)}, u32[]{:S(2)}) %collective-permute-start.5) | collective-permute-done | bytes 131104 | tf_op jit(solution)/shard_map/ppermute | solution.py:599
  42.5 3.8 %collective-permute-done.6.two_ref = bf16[2,2,128,128]{3,2,1,0:T(8,128)(2,1)S(1)} collective-permute-done((bf16[2,2,128,128]{3,2,1,0:T(8,128)(2,1)S(1)}, bf16[2,2,128,128]{3,2,1,0:T(8,128)(2,1)S(1)}, u32[]{:S(2)}, u32[]{:S(2)}) %collective-permute-start.6) | collective-permute-done | bytes 131104 | tf_op jit(solution)/shard_map/ppermute | solution.py:599
  46.3 4.4 %back.1 = (bf16[2,256,896]{2,1,0:T(8,128)(2,1)S(1)}, f32[16,128]{1,0:T(8,128)S(1)}) custom-call(s32[6]{0:T(128)S(1)} %copy-done.6, f32[4,3,256,128]{3,2,1,0:T(8,128)S(1)} %copy-done.11, f32[4,4,256,128]{3,2,1,0:T(8,128)S(1)} %extra.1.extra_ref, f32[4,256,128]{2,1,0:T(8,128)S(1)} %get-tuple-element.40.gates_ref, ...), custom_call_target="tpu_custom_call" | custom-call | flops 4000000000 | bytes 8000000 | tf_op jit(solution)/shard_map/back/pallas_call | solution.py:200
  50.7 1.8 %give.1 = (bf16[576,768]{1,0:T(8,128)(2,1)S(1)}, bf16[272,768]{1,0:T(8,128)(2,1)S(1)}, bf16[272,768]{1,0:T(8,128)(2,1)S(1)}, bf16[272,768]{1,0:T(8,128)(2,1)S(1)}) custom-call(s32[6]{0:T(128)S(1)} %copy-done.6, bf16[2,4,4,64,512]{4,3,2,1,0:T(8,128)(2,1)S(1)} %flip.1.after_ref.flipped_ref, bf16[2,256,896]{2,1,0:T(8,128)(2,1)S(1)} %get-tuple-element.47.grads_ref.mine_ref, ...), custom_call_target="tpu_custom_call" | custom-call | flops 1000000000 | bytes 4000000 | tf_op jit(solution)/shard_map/give/pallas_call | solution.py:401
  52.6 1.4 %collective-permute-start.15 = (bf16[272,768]{1,0:T(8,128)(2,1)S(1)}, bf16[272,768]{1,0:T(8,128)(2,1)S(1)}, u32[]{:S(2)}, u32[]{:S(2)}) collective-permute-start(bf16[272,768]{1,0:T(8,128)(2,1)S(1)} %get-tuple-element.58), channel_id=1, source_target_pairs={{0,36},{4,8},{8,44},{12,16},{16,52},{20,24},{24,60},{28,0},{32,68}... | collective-permute-start | bytes 1253384 | tf_op jit(solution)/shard_map/ppermute | solution.py:649
  54.0 0.9 collective-permute-start.16
  55.0 1.2 %collective-permute-start.17 = (bf16[272,768]{1,0:T(8,128)(2,1)S(1)}, bf16[272,768]{1,0:T(8,128)(2,1)S(1)}, u32[]{:S(2)}, u32[]{:S(2)}) collective-permute-start(bf16[272,768]{1,0:T(8,128)(2,1)S(1)} %get-tuple-element.60), channel_id=1, source_target_pairs={{0,68},{4,16},{8,76},{12,24},{16,84},{20,0},{24,92},{28,8},{32,100... | collective-permute-start | bytes 1253384 | tf_op jit(solution)/shard_map/ppermute | solution.py:649
  56.2 1.8 %keep.1 = (bf16[272,768]{1,0:T(8,128)(2,1)S(1)}, bf16[272,768]{1,0:T(8,128)(2,1)S(1)}, bf16[272,768]{1,0:T(8,128)(2,1)S(1)}, bf16[272,768]{1,0:T(8,128)(2,1)S(1)}) custom-call(s32[6]{0:T(128)S(1)} %copy-done.6, bf16[2,4,4,64,512]{4,3,2,1,0:T(8,128)(2,1)S(1)} %flip.1.after_ref.flipped_ref, bf16[2,256,896]{2,1,0:T(8,128)(2,1)S(1)} %get-tuple-element.47.grads_ref.mine_ref, ...), custom_call_target="tpu_custom_call" | custom-call | flops 1000000000 | bytes 4000000 | tf_op jit(solution)/shard_map/keep/pallas_call | solution.py:401
  57.9 2.2 %collective-permute-start.13 = (bf16[272,768]{1,0:T(8,128)(2,1)S(1)}, bf16[272,768]{1,0:T(8,128)(2,1)S(1)}, u32[]{:S(2)}, u32[]{:S(2)}) collective-permute-start(bf16[272,768]{1,0:T(8,128)(2,1)S(1)} %get-tuple-element.56), channel_id=1, source_target_pairs={{0,24},{4,100},{8,0},{12,108},{16,8},{20,116},{24,16},{28,124},{32... | collective-permute-start | bytes 1253384 | tf_op jit(solution)/shard_map/ppermute | solution.py:599
  60.1 1.9 %collective-permute-start.14 = (bf16[272,768]{1,0:T(8,128)(2,1)S(1)}, bf16[272,768]{1,0:T(8,128)(2,1)S(1)}, u32[]{:S(2)}, u32[]{:S(2)}) collective-permute-start(bf16[272,768]{1,0:T(8,128)(2,1)S(1)} %get-tuple-element.57), channel_id=1, source_target_pairs={{0,16},{4,68},{8,24},{12,76},{16,0},{20,84},{24,8},{28,92},{32,48}... | collective-permute-start | bytes 1253384 | tf_op jit(solution)/shard_map/ppermute | solution.py:599
  62.1 8.2 %collective-permute-done.15.refs_5_ = bf16[272,768]{1,0:T(8,128)(2,1)S(1)} collective-permute-done((bf16[272,768]{1,0:T(8,128)(2,1)S(1)}, bf16[272,768]{1,0:T(8,128)(2,1)S(1)}, u32[]{:S(2)}, u32[]{:S(2)}) %collective-permute-start.15) | collective-permute-done | bytes 417824 | tf_op jit(solution)/shard_map/ppermute | solution.py:649
  70.3 3.4 %inputs.1 = (bf16[256,512]{1,0:T(8,128)(2,1)S(1)}, bf16[256,512]{1,0:T(8,128)(2,1)S(1)}, bf16[256,512]{1,0:T(8,128)(2,1)S(1)}, bf16[256,512]{1,0:T(8,128)(2,1)S(1)}) custom-call(s32[6]{0:T(128)S(1)} %copy-done.6, bf16[2,256,896]{2,1,0:T(8,128)(2,1)S(1)} %get-tuple-element.47.grads_ref.mine_ref, ...), custom_call_target="tpu_custom_call" | custom-call | flops 40000000000 | bytes 8000000 | tf_op jit(solution)/shard_map/inputs/pallas_call | solution.py:661
  73.7 2.0 %collective-permute-start.9 = (bf16[256,512]{1,0:T(8,128)(2,1)S(1)}, bf16[256,512]{1,0:T(8,128)(2,1)S(1)}, u32[]{:S(2)}, u32[]{:S(2)}) collective-permute-start(bf16[256,512]{1,0:T(8,128)(2,1)S(1)} %get-tuple-element.52), channel_id=1, source_target_pairs={{0,1},{1,2},{2,3},{3,0},{4,5},{5,6},{6,7},{7,4},{8,9},{9,10},{10,1... | collective-permute-start | bytes 786440 | tf_op jit(solution)/shard_map/ppermute | solution.py:683
  75.7 3.6 %collective-permute-start.10 = (bf16[256,512]{1,0:T(8,128)(2,1)S(1)}, bf16[256,512]{1,0:T(8,128)(2,1)S(1)}, u32[]{:S(2)}, u32[]{:S(2)}) collective-permute-start(bf16[256,512]{1,0:T(8,128)(2,1)S(1)} %get-tuple-element.53), channel_id=1, source_target_pairs={{0,2},{1,3},{2,0},{3,1},{4,6},{5,7},{6,4},{7,5},{8,10},{9,11},{10,... | collective-permute-start | bytes 786440 | tf_op jit(solution)/shard_map/ppermute | solution.py:683
  79.3 1.0 %collective-permute-start.11 = (bf16[256,512]{1,0:T(8,128)(2,1)S(1)}, bf16[256,512]{1,0:T(8,128)(2,1)S(1)}, u32[]{:S(2)}, u32[]{:S(2)}) collective-permute-start(bf16[256,512]{1,0:T(8,128)(2,1)S(1)} %get-tuple-element.54), channel_id=1, source_target_pairs={{0,3},{1,0},{2,1},{3,2},{4,7},{5,4},{6,5},{7,6},{8,11},{9,8},{10,9... | collective-permute-start | bytes 786440 | tf_op jit(solution)/shard_map/ppermute | solution.py:683
  80.3 1.1 %middle.1 = (f32[2,80,768]{2,1,0:T(8,128)S(1)}, bf16[2,80,768]{2,1,0:T(8,128)(2,1)S(1)}, bf16[2,80,768]{2,1,0:T(8,128)(2,1)S(1)}, bf16[2,80,768]{2,1,0:T(8,128)(2,1)S(1)}) custom-call(s32[6]{0:T(128)S(1)} %copy-done.6, bf16[272,768]{1,0:T(8,128)(2,1)S(1)} %get-tuple-element.55.refs_0_, bf16[272,768]{1,0:T(8,128)(2,1)S(1)} %collective-permute-done.12.refs_1_, ...), custom_call_target="tpu_custom_call" | custom-call | tf_op jit(solution)/shard_map/middle/pallas_call | solution.py:485
  81.4 1.4 %collective-permute-start.18 = (bf16[2,80,768]{2,1,0:T(8,128)(2,1)S(1)}, bf16[2,80,768]{2,1,0:T(8,128)(2,1)S(1)}, u32[]{:S(2)}, u32[]{:S(2)}) collective-permute-start(bf16[2,80,768]{2,1,0:T(8,128)(2,1)S(1)} %get-tuple-element.62), channel_id=1, source_target_pairs={{0,32},{4,12},{8,40},{12,20},{16,48},{20,28},{24,56},{28,4},{32,64... | collective-permute-start | bytes 737288 | tf_op jit(solution)/shard_map/ppermute | solution.py:599
  82.8 1.9 %collective-permute-start.19 = (bf16[2,80,768]{2,1,0:T(8,128)(2,1)S(1)}, bf16[2,80,768]{2,1,0:T(8,128)(2,1)S(1)}, u32[]{:S(2)}, u32[]{:S(2)}) collective-permute-start(bf16[2,80,768]{2,1,0:T(8,128)(2,1)S(1)} %get-tuple-element.63), channel_id=1, source_target_pairs={{0,96},{4,28},{8,104},{12,4},{16,112},{20,12},{24,120},{28,20},{32... | collective-permute-start | bytes 737288 | tf_op jit(solution)/shard_map/ppermute | solution.py:599
  84.7 1.5 %collective-permute-start.20 = (bf16[2,80,768]{2,1,0:T(8,128)(2,1)S(1)}, bf16[2,80,768]{2,1,0:T(8,128)(2,1)S(1)}, u32[]{:S(2)}, u32[]{:S(2)}) collective-permute-start(bf16[2,80,768]{2,1,0:T(8,128)(2,1)S(1)} %get-tuple-element.64), channel_id=1, source_target_pairs={{0,64},{4,20},{8,72},{12,28},{16,80},{20,4},{24,88},{28,12},{32,96... | collective-permute-start | bytes 737288 | tf_op jit(solution)/shard_map/ppermute | solution.py:599
  86.2 0.3 collective-permute-done.10
  86.5 0.9 collective-permute-done.11
  87.4 0.1 add_convert_fusion.after_ref
  87.5 1.3 %collective-permute-done.18.one_ref = bf16[2,80,768]{2,1,0:T(8,128)(2,1)S(1)} collective-permute-done((bf16[2,80,768]{2,1,0:T(8,128)(2,1)S(1)}, bf16[2,80,768]{2,1,0:T(8,128)(2,1)S(1)}, u32[]{:S(2)}, u32[]{:S(2)}) %collective-permute-start.18) | collective-permute-done | bytes 245792 | tf_op jit(solution)/shard_map/ppermute | solution.py:599
  88.9 2.2 %collective-permute-done.19.two_ref = bf16[2,80,768]{2,1,0:T(8,128)(2,1)S(1)} collective-permute-done((bf16[2,80,768]{2,1,0:T(8,128)(2,1)S(1)}, bf16[2,80,768]{2,1,0:T(8,128)(2,1)S(1)}, u32[]{:S(2)}, u32[]{:S(2)}) %collective-permute-start.19) | collective-permute-done | bytes 245792 | tf_op jit(solution)/shard_map/ppermute | solution.py:599
  91.1 1.3 %collective-permute-done.20.three_ref = bf16[2,80,768]{2,1,0:T(8,128)(2,1)S(1)} collective-permute-done((bf16[2,80,768]{2,1,0:T(8,128)(2,1)S(1)}, bf16[2,80,768]{2,1,0:T(8,128)(2,1)S(1)}, u32[]{:S(2)}, u32[]{:S(2)}) %collective-permute-start.20) | collective-permute-done | bytes 245792 | tf_op jit(solution)/shard_map/ppermute | solution.py:599
  92.4 1.3 %total.1 = (f32[64,512]{1,0:T(8,128)}, f32[64,512]{1,0:T(8,128)}, f32[64,512]{1,0:T(8,128)}, f32[4,64]{1,0:T(4,128)}, f32[16,128]{1,0:T(8,128)S(1)}) custom-call(s32[6]{0:T(128)S(1)} %copy-done.6, f32[2,80,768]{2,1,0:T(8,128)S(1)} %get-tuple-element.61.own_ref, bf16[2,80,768]{2,1,0:T(8,128)(2,1)S(1)} %collective-permute-done.18.one_ref, ...), custom_call_target="tpu_custom_call" | custom-call | tf_op jit(solution)/shard_map/total/pallas_call | solution.py:485
  93.8 1.2 %collective-permute-done.21 = f32[16,128]{1,0:T(8,128)S(1)} collective-permute-done((f32[16,128]{1,0:T(8,128)S(1)}, f32[16,128]{1,0:T(8,128)S(1)}, u32[]{:S(2)}, u32[]{:S(2)}) %collective-permute-start.21) | collective-permute-done | bytes 8224 | tf_op jit(solution)/shard_map/ppermute | solution.py:540
  94.9 0.6 fusion
  (36 shorter events, 0.2 us)
Async XLA Ops:
  0.6 6.4 %collective-permute-start = (bf16[256,2048]{1,0:T(8,128)(2,1)}, bf16[256,2048]{1,0:T(8,128)(2,1)S(1)}, u32[]{:S(2)}, u32[]{:S(2)}) collective-permute-start(bf16[256,2048]{1,0:T(8,128)(2,1)} %own_ref.1), channel_id=1, source_target_pairs={{0,4},{4,0},{8,12},{12,8},{16,20},{20,16},{24,28},{28,24},{32,36},... | collective-permute-start | bytes 3145736 | tf_op jit(solution)/shard_map/ppermute | solution.py:540
  0.7 6.3 %collective-permute-start.1 = (bf16[256,512]{1,0:T(8,128)(2,1)}, bf16[256,512]{1,0:T(8,128)(2,1)S(1)}, u32[]{:S(2)}, u32[]{:S(2)}) collective-permute-start(bf16[256,512]{1,0:T(8,128)(2,1)} %do_ref.5), channel_id=1, source_target_pairs={{0,4},{4,0},{8,12},{12,8},{16,20},{20,16},{24,28},{28,24},{32,36},... | collective-permute-start | bytes 786440 | tf_op jit(solution)/shard_map/ppermute | solution.py:540
  1.9 5.2 %copy-start.6 = (s32[6]{0:T(128)S(1)}, s32[6]{0:T(128)}, u32[]{:S(2)}) copy-start(s32[6]{0:T(128)} %stack.27.place_ref.core_ref) | copy-start | bytes 76
  1.9 5.2 %copy-start.7 = (bf16[2048,4]{0,1:T(4,128)(2,1)S(1)}, bf16[2048,4]{0,1:T(4,128)(2,1)}, u32[]{:S(2)}) copy-start(bf16[2048,4]{0,1:T(4,128)(2,1)} %param.11) | copy-start | bytes 49156
  1.9 5.2 %copy-start.8 = (bf16[256,512]{1,0:T(8,128)(2,1)S(1)}, bf16[256,512]{1,0:T(8,128)(2,1)}, u32[]{:S(2)}) copy-start(bf16[256,512]{1,0:T(8,128)(2,1)} %do_ref.5) | copy-start | bytes 786436
  1.9 5.2 %copy-start.9 = (f32[4]{0:T(128)S(1)}, f32[4]{0:T(128)}, u32[]{:S(2)}) copy-start(f32[4]{0:T(128)} %bb_ref.1) | copy-start | bytes 52
  7.1 1.2 %copy-start.5 = (f32[256,896]{1,0:T(8,128)S(1)}, f32[256,896]{1,0:T(8,128)}, u32[]{:S(2)}) copy-start(f32[256,896]{1,0:T(8,128)} %project.1.own_ref) | copy-start | bytes 2752516
  18.5 11.7 %collective-permute-start.4 = (bf16[2,3,128,128]{3,2,1,0:T(8,128)(2,1)S(1)}, bf16[2,3,128,128]{3,2,1,0:T(8,128)(2,1)S(1)}, u32[]{:S(2)}, u32[]{:S(2)}) collective-permute-start(bf16[2,3,128,128]{3,2,1,0:T(8,128)(2,1)S(1)} %get-tuple-element.42.after_ref.own_ref), channel_id=1, source_target_pairs={{0,24},{4,28},{8,0},{12,4},{16,8},{20,12},{24,16},{28,20},{32,56},... | collective-permute-start | bytes 589832 | tf_op jit(solution)/shard_map/ppermute | solution.py:599
  21.6 9.3 %collective-permute-start.3 = (bf16[2,3,128,128]{3,2,1,0:T(8,128)(2,1)S(1)}, bf16[2,3,128,128]{3,2,1,0:T(8,128)(2,1)S(1)}, u32[]{:S(2)}, u32[]{:S(2)}) collective-permute-start(bf16[2,3,128,128]{3,2,1,0:T(8,128)(2,1)S(1)} %get-tuple-element.42.after_ref.own_ref), channel_id=1, source_target_pairs={{0,16},{4,20},{8,24},{12,28},{16,0},{20,4},{24,8},{28,12},{32,48},... | collective-permute-start | bytes 589832 | tf_op jit(solution)/shard_map/ppermute | solution.py:599
  22.2 11.7 %collective-permute-start.2 = (bf16[2,3,128,128]{3,2,1,0:T(8,128)(2,1)S(1)}, bf16[2,3,128,128]{3,2,1,0:T(8,128)(2,1)S(1)}, u32[]{:S(2)}, u32[]{:S(2)}) collective-permute-start(bf16[2,3,128,128]{3,2,1,0:T(8,128)(2,1)S(1)} %get-tuple-element.42.after_ref.own_ref), channel_id=1, source_target_pairs={{0,8},{4,12},{8,16},{12,20},{16,24},{20,28},{24,0},{28,4},{32,40},... | collective-permute-start | bytes 589832 | tf_op jit(solution)/shard_map/ppermute | solution.py:599
  23.2 1.4 %copy-start.10 = (f32[4,3,256,128]{3,2,1,0:T(8,128)S(1)}, f32[4,3,256,128]{3,2,1,0:T(8,128)}, u32[]{:S(2)}) copy-start(f32[4,3,256,128]{3,2,1,0:T(8,128)} %get-tuple-element.38.saved_ref) | copy-start | bytes 4718596
  24.6 1.6 %copy-start.12 = (bf16[4,4,256,256]{3,2,1,0:T(8,128)(2,1)S(1)}, bf16[4,4,256,256]{3,2,1,0:T(8,128)(2,1)}, u32[]{:S(2)}) copy-start(bf16[4,4,256,256]{3,2,1,0:T(8,128)(2,1)} %get-tuple-element.39.solve_ref) | copy-start | bytes 6291460
  26.2 2.7 %copy-start = (bf16[256,2048]{1,0:T(8,128)(2,1)S(1)}, bf16[256,2048]{1,0:T(8,128)(2,1)}, u32[]{:S(2)}) copy-start(bf16[256,2048]{1,0:T(8,128)(2,1)} %own_ref.1) | copy-start | bytes 3145732
  29.9 16.4 %copy-start.11 = (f32[4,3,256,128]{3,2,1,0:T(8,128)S(1)}, f32[4,3,256,128]{3,2,1,0:T(8,128)}, u32[]{:S(2)}) copy-start(f32[4,3,256,128]{3,2,1,0:T(8,128)} %get-tuple-element.38.saved_ref) | copy-start | bytes 4718596
  35.8 6.7 %collective-permute-start.5 = (bf16[2,2,128,128]{3,2,1,0:T(8,128)(2,1)S(1)}, bf16[2,2,128,128]{3,2,1,0:T(8,128)(2,1)S(1)}, u32[]{:S(2)}, u32[]{:S(2)}) collective-permute-start(bf16[2,2,128,128]{3,2,1,0:T(8,128)(2,1)S(1)} %get-tuple-element.44), channel_id=1, source_target_pairs={{0,32},{4,36},{8,40},{12,44},{16,48},{20,52},{24,56},{28,60},{32,6... | collective-permute-start | bytes 393224 | tf_op jit(solution)/shard_map/ppermute | solution.py:599
  37.4 8.9 %collective-permute-start.6 = (bf16[2,2,128,128]{3,2,1,0:T(8,128)(2,1)S(1)}, bf16[2,2,128,128]{3,2,1,0:T(8,128)(2,1)S(1)}, u32[]{:S(2)}, u32[]{:S(2)}) collective-permute-start(bf16[2,2,128,128]{3,2,1,0:T(8,128)(2,1)S(1)} %get-tuple-element.45), channel_id=1, source_target_pairs={{0,64},{4,68},{8,72},{12,76},{16,80},{20,84},{24,88},{28,92},{32,9... | collective-permute-start | bytes 393224 | tf_op jit(solution)/shard_map/ppermute | solution.py:599
  40.1 6.2 %collective-permute-start.7 = (bf16[2,2,128,128]{3,2,1,0:T(8,128)(2,1)S(1)}, bf16[2,2,128,128]{3,2,1,0:T(8,128)(2,1)S(1)}, u32[]{:S(2)}, u32[]{:S(2)}) collective-permute-start(bf16[2,2,128,128]{3,2,1,0:T(8,128)(2,1)S(1)} %get-tuple-element.46), channel_id=1, source_target_pairs={{0,96},{4,100},{8,104},{12,108},{16,112},{20,116},{24,120},{28,124... | collective-permute-start | bytes 393224 | tf_op jit(solution)/shard_map/ppermute | solution.py:599
  50.7 19.6 %copy-start.2 = (bf16[2048,512]{1,0:T(8,128)(2,1)S(1)}, bf16[2048,512]{1,0:T(8,128)(2,1)}, u32[]{:S(2)}) copy-start(bf16[2048,512]{1,0:T(8,128)(2,1)} %wk_ref.5) | copy-start | bytes 6291460
  50.7 19.6 %copy-start.3 = (bf16[2048,512]{1,0:T(8,128)(2,1)S(1)}, bf16[2048,512]{1,0:T(8,128)(2,1)}, u32[]{:S(2)}) copy-start(bf16[2048,512]{1,0:T(8,128)(2,1)} %wv_ref.5) | copy-start | bytes 6291460
  52.5 17.8 %copy-start.1 = (bf16[2048,512]{1,0:T(8,128)(2,1)S(1)}, bf16[2048,512]{1,0:T(8,128)(2,1)}, u32[]{:S(2)}) copy-start(bf16[2048,512]{1,0:T(8,128)(2,1)} %wq_ref.5) | copy-start | bytes 6291460
  52.5 3.7 %collective-permute-start.8 = (bf16[576,768]{1,0:T(8,128)(2,1)S(1)}, bf16[576,768]{1,0:T(8,128)(2,1)S(1)}, u32[]{:S(2)}, u32[]{:S(2)}) collective-permute-start(bf16[576,768]{1,0:T(8,128)(2,1)S(1)} %get-tuple-element.49), channel_id=1, source_target_pairs={{0,4},{4,0},{8,12},{12,8},{16,20},{20,16},{24,28},{28,24},{32,36},... | collective-permute-start | bytes 2654216 | tf_op jit(solution)/shard_map/ppermute | solution.py:649
  52.6 17.7 %collective-permute-start.15 = (bf16[272,768]{1,0:T(8,128)(2,1)S(1)}, bf16[272,768]{1,0:T(8,128)(2,1)S(1)}, u32[]{:S(2)}, u32[]{:S(2)}) collective-permute-start(bf16[272,768]{1,0:T(8,128)(2,1)S(1)} %get-tuple-element.58), channel_id=1, source_target_pairs={{0,36},{4,8},{8,44},{12,16},{16,52},{20,24},{24,60},{28,0},{32,68}... | collective-permute-start | bytes 1253384 | tf_op jit(solution)/shard_map/ppermute | solution.py:649
  54.0 19.7 %collective-permute-start.16 = (bf16[272,768]{1,0:T(8,128)(2,1)S(1)}, bf16[272,768]{1,0:T(8,128)(2,1)S(1)}, u32[]{:S(2)}, u32[]{:S(2)}) collective-permute-start(bf16[272,768]{1,0:T(8,128)(2,1)S(1)} %get-tuple-element.59), channel_id=1, source_target_pairs={{0,100},{4,24},{8,108},{12,0},{16,116},{20,8},{24,124},{28,16},{32... | collective-permute-start | bytes 1253384 | tf_op jit(solution)/shard_map/ppermute | solution.py:649
  55.0 20.8 %collective-permute-start.17 = (bf16[272,768]{1,0:T(8,128)(2,1)S(1)}, bf16[272,768]{1,0:T(8,128)(2,1)S(1)}, u32[]{:S(2)}, u32[]{:S(2)}) collective-permute-start(bf16[272,768]{1,0:T(8,128)(2,1)S(1)} %get-tuple-element.60), channel_id=1, source_target_pairs={{0,68},{4,16},{8,76},{12,24},{16,84},{20,0},{24,92},{28,8},{32,100... | collective-permute-start | bytes 1253384 | tf_op jit(solution)/shard_map/ppermute | solution.py:649
  57.9 21.4 %collective-permute-start.13 = (bf16[272,768]{1,0:T(8,128)(2,1)S(1)}, bf16[272,768]{1,0:T(8,128)(2,1)S(1)}, u32[]{:S(2)}, u32[]{:S(2)}) collective-permute-start(bf16[272,768]{1,0:T(8,128)(2,1)S(1)} %get-tuple-element.56), channel_id=1, source_target_pairs={{0,24},{4,100},{8,0},{12,108},{16,8},{20,116},{24,16},{28,124},{32... | collective-permute-start | bytes 1253384 | tf_op jit(solution)/shard_map/ppermute | solution.py:599
  60.1 20.2 %collective-permute-start.14 = (bf16[272,768]{1,0:T(8,128)(2,1)S(1)}, bf16[272,768]{1,0:T(8,128)(2,1)S(1)}, u32[]{:S(2)}, u32[]{:S(2)}) collective-permute-start(bf16[272,768]{1,0:T(8,128)(2,1)S(1)} %get-tuple-element.57), channel_id=1, source_target_pairs={{0,16},{4,68},{8,24},{12,76},{16,0},{20,84},{24,8},{28,92},{32,48}... | collective-permute-start | bytes 1253384 | tf_op jit(solution)/shard_map/ppermute | solution.py:599
  70.3 10.1 %collective-permute-start.12 = (bf16[272,768]{1,0:T(8,128)(2,1)S(1)}, bf16[272,768]{1,0:T(8,128)(2,1)S(1)}, u32[]{:S(2)}, u32[]{:S(2)}) collective-permute-start(bf16[272,768]{1,0:T(8,128)(2,1)S(1)} %get-tuple-element.50.after_ref), channel_id=1, source_target_pairs={{0,8},{4,36},{8,16},{12,44},{16,24},{20,52},{24,0},{28,60},{32,40}... | collective-permute-start | bytes 1253384 | tf_op jit(solution)/shard_map/ppermute | solution.py:599
  73.7 11.0 %collective-permute-start.9 = (bf16[256,512]{1,0:T(8,128)(2,1)S(1)}, bf16[256,512]{1,0:T(8,128)(2,1)S(1)}, u32[]{:S(2)}, u32[]{:S(2)}) collective-permute-start(bf16[256,512]{1,0:T(8,128)(2,1)S(1)} %get-tuple-element.52), channel_id=1, source_target_pairs={{0,1},{1,2},{2,3},{3,0},{4,5},{5,6},{6,7},{7,4},{8,9},{9,10},{10,1... | collective-permute-start | bytes 786440 | tf_op jit(solution)/shard_map/ppermute | solution.py:683
  75.7 10.7 %collective-permute-start.10 = (bf16[256,512]{1,0:T(8,128)(2,1)S(1)}, bf16[256,512]{1,0:T(8,128)(2,1)S(1)}, u32[]{:S(2)}, u32[]{:S(2)}) collective-permute-start(bf16[256,512]{1,0:T(8,128)(2,1)S(1)} %get-tuple-element.53), channel_id=1, source_target_pairs={{0,2},{1,3},{2,0},{3,1},{4,6},{5,7},{6,4},{7,5},{8,10},{9,11},{10,... | collective-permute-start | bytes 786440 | tf_op jit(solution)/shard_map/ppermute | solution.py:683
  79.3 8.1 %collective-permute-start.11 = (bf16[256,512]{1,0:T(8,128)(2,1)S(1)}, bf16[256,512]{1,0:T(8,128)(2,1)S(1)}, u32[]{:S(2)}, u32[]{:S(2)}) collective-permute-start(bf16[256,512]{1,0:T(8,128)(2,1)S(1)} %get-tuple-element.54), channel_id=1, source_target_pairs={{0,3},{1,0},{2,1},{3,2},{4,7},{5,4},{6,5},{7,6},{8,11},{9,8},{10,9... | collective-permute-start | bytes 786440 | tf_op jit(solution)/shard_map/ppermute | solution.py:683
  81.4 7.5 %collective-permute-start.18 = (bf16[2,80,768]{2,1,0:T(8,128)(2,1)S(1)}, bf16[2,80,768]{2,1,0:T(8,128)(2,1)S(1)}, u32[]{:S(2)}, u32[]{:S(2)}) collective-permute-start(bf16[2,80,768]{2,1,0:T(8,128)(2,1)S(1)} %get-tuple-element.62), channel_id=1, source_target_pairs={{0,32},{4,12},{8,40},{12,20},{16,48},{20,28},{24,56},{28,4},{32,64... | collective-permute-start | bytes 737288 | tf_op jit(solution)/shard_map/ppermute | solution.py:599
  82.8 8.3 %collective-permute-start.19 = (bf16[2,80,768]{2,1,0:T(8,128)(2,1)S(1)}, bf16[2,80,768]{2,1,0:T(8,128)(2,1)S(1)}, u32[]{:S(2)}, u32[]{:S(2)}) collective-permute-start(bf16[2,80,768]{2,1,0:T(8,128)(2,1)S(1)} %get-tuple-element.63), channel_id=1, source_target_pairs={{0,96},{4,28},{8,104},{12,4},{16,112},{20,12},{24,120},{28,20},{32... | collective-permute-start | bytes 737288 | tf_op jit(solution)/shard_map/ppermute | solution.py:599
  84.7 7.7 %collective-permute-start.20 = (bf16[2,80,768]{2,1,0:T(8,128)(2,1)S(1)}, bf16[2,80,768]{2,1,0:T(8,128)(2,1)S(1)}, u32[]{:S(2)}, u32[]{:S(2)}) collective-permute-start(bf16[2,80,768]{2,1,0:T(8,128)(2,1)S(1)} %get-tuple-element.64), channel_id=1, source_target_pairs={{0,64},{4,20},{8,72},{12,28},{16,80},{20,4},{24,88},{28,12},{32,96... | collective-permute-start | bytes 737288 | tf_op jit(solution)/shard_map/ppermute | solution.py:599
  87.5 8.0 %copy-start.4 = (bf16[256,512]{1,0:T(8,128)(2,1)}, bf16[256,512]{1,0:T(8,128)(2,1)S(1)}, u32[]{:S(2)}) copy-start(bf16[256,512]{1,0:T(8,128)(2,1)S(1)} %add_convert_fusion.after_ref) | copy-start | bytes 786436
  93.8 1.2 %collective-permute-start.21 = (f32[16,128]{1,0:T(8,128)S(1)}, f32[16,128]{1,0:T(8,128)S(1)}, u32[]{:S(2)}, u32[]{:S(2)}) collective-permute-start(f32[16,128]{1,0:T(8,128)S(1)} %get-tuple-element.69), channel_id=1, source_target_pairs={{0,4},{4,0},{8,12},{12,8},{16,20},{20,16},{24,28},{28,24},{32,36},... | collective-permute-start | bytes 24584 | tf_op jit(solution)/shard_map/ppermute | solution.py:540
